TPU v7x, 512 devices: a whole 4x8x8 slice. The times are simulated.
512 devices in a mesh: dp: 16 (over z, core), cent: 32 (over x, y).
Axes of the slice: x: 4, y: 8, z: 8, core: 2. Of those that a mesh axis runs over, the one named last changes fastest.
Arguments:
- tokens: bfloat16 [32768, 128], P('dp'), may hold values from -6 to 20
- centroids: bfloat16 [16384, 128], P('cent'), may hold values from -6 to 6
- diagonal_factors: float32 [128], replicated, may hold values from 0.5 to 2
Outputs:
- new_centroids: float32 [16384, 128], P('cent')
- masses: float32 [16384], P('cent')
All inputs are finite; a program needn't handle non-finite values.
Results may differ from a plain program's by a relative error of at most 0.0076.
Values sent between devices are 32-bit elements; how exact they have to be, the bound alone decides.
No kernel may reach another device: no remote copies, remote signals or barrier semaphores. Data moves between devices by JAX's collectives and lax.ppermute only.
A program may use at most 64 MiB of HBM per device.

v0:
```python
import math

import jax
import jax.numpy as jnp
from jax import lax
from jax.sharding import PartitionSpec as P

ITERS = 3


entropic_smoothing_factor = 4.0


def quadratic_separation(tokens, rescaled_penalty, cluster_center_length_power, diagonal_factors):
    tok_float = tokens.astype(jnp.float32)
    tok_norm = jnp.sum(tok_float * tok_float * diagonal_factors[None, :], axis=1)
    cross = lax.dot_general(
        tokens, rescaled_penalty, (((1,), (1,)), ((), ())), preferred_element_type=jnp.float32
    )
    return tok_norm[:, None] + cluster_center_length_power[None, :] - 2.0 * cross


def source_side_softmaximum(unnormalized_affinity):
    top = lax.pmax(jnp.max(unnormalized_affinity, axis=1), "cent")
    total = lax.psum(jnp.sum(jnp.exp(unnormalized_affinity - top[:, None]), axis=1), "cent")
    return top + jnp.log(total)


def column_logsumexp(unnormalized_affinity):
    top = lax.pmax(jnp.max(unnormalized_affinity, axis=0), "dp")
    total = lax.psum(jnp.sum(jnp.exp(unnormalized_affinity - top[None, :]), axis=0), "dp")
    return top + jnp.log(total)


def shards(tokens, centroids, diagonal_factors):
    tok_count = tokens.shape[0] * lax.axis_size("dp")
    cent_count = centroids.shape[0] * lax.axis_size("cent")
    cent_float = centroids.astype(jnp.float32)
    rescaled_penalty = (cent_float * diagonal_factors[None, :]).astype(jnp.bfloat16)
    cluster_center_length_power = jnp.sum(
        cent_float * cent_float * diagonal_factors[None, :], axis=1
    )

    def existing_cluster_centers():
        return quadratic_separation(
            tokens, rescaled_penalty, cluster_center_length_power, diagonal_factors
        )

    source_mass_logarithm = -math.log(tok_count)
    target_mass_logarithm = -math.log(cent_count)
    source_side_multiplier = jnp.zeros((tokens.shape[0],), jnp.float32)
    target_side_multiplier = jnp.zeros((centroids.shape[0],), jnp.float32)
    for iteration in range(ITERS):
        unnormalized_affinity = (
            source_side_multiplier[:, None] - existing_cluster_centers()
        ) / entropic_smoothing_factor
        target_side_multiplier = entropic_smoothing_factor * (
            target_mass_logarithm - column_logsumexp(unnormalized_affinity)
        )
        unnormalized_affinity = (
            target_side_multiplier[None, :] - existing_cluster_centers()
        ) / entropic_smoothing_factor
        source_side_multiplier = entropic_smoothing_factor * (
            source_mass_logarithm - source_side_softmaximum(unnormalized_affinity)
        )
    assignment_share = jnp.exp(
        (
            source_side_multiplier[:, None]
            + target_side_multiplier[None, :]
            - existing_cluster_centers()
        )
        / entropic_smoothing_factor
        + math.log(tok_count)
    )
    mass_part = jnp.sum(assignment_share, axis=0)
    numer_part = lax.dot_general(
        assignment_share.astype(jnp.bfloat16),
        tokens,
        (((0,), (0,)), ((), ())),
        preferred_element_type=jnp.float32,
    )
    ratio = cent_count / tok_count
    numer, mass = lax.psum((numer_part, mass_part), "dp")
    new_centroids = numer / mass[:, None]
    masses = mass * ratio
    return (new_centroids, masses)


def solution(mesh):
    return jax.shard_map(
        shards,
        mesh=mesh,
        in_specs=(P("dp", None), P("cent", None), P()),
        out_specs=(P("cent", None), P("cent")),
        check_vma=False,
    )
```

profile of v0, /device:TPU:1, one launch (start us, length us, event | category | flops | bytes accessed | tf_op | source)
XLA Modules:
  0.0 747.9 jit_solution(11160008986901668493)
XLA Ops:
  7.2 0.0 all-reduce.2.cloned.1.call-start
  7.2 1.1 fusion.11
  8.3 1.4 multiply_reduce_fusion
  9.7 4.1 fusion
  13.7 30.6 %pmax.42 = f32[512]{0:T(512)S(1)} all-reduce(f32[512]{0:T(512)S(1)} %get-tuple-element.2), channel_id=1, replica_groups=mesh['dp'=16,'cent'=32] {'dp'}, use_global_device_ids=true, to_apply=%region_3.0 | all-reduce | flops 512 | bytes 4096 | tf_op jit(solution)/shard_map/pmax | solution.py:30
  44.3 3.1 exponential_reduce_fusion.5
  47.4 25.8 %psum.56 = f32[512]{0:T(512)S(1)} all-reduce(f32[512]{0:T(512)S(1)} %exponential_reduce_fusion.5), channel_id=1, replica_groups=mesh['dp'=16,'cent'=32] {'dp'}, use_global_device_ids=true, to_apply=%region_5.0 | all-reduce | flops 512 | bytes 4096 | tf_op jit(solution)/shard_map/psum | solution.py:31
  73.2 2.7 fusion.1
  75.9 62.3 %pmax.43 = f32[2048]{0:T(1024)S(1)} all-reduce(f32[2048]{0:T(1024)S(1)} %fusion.1), channel_id=1, replica_groups=mesh['dp'=16,'cent'=32] {'cent'}, use_global_device_ids=true, to_apply=%region_7.0 | all-reduce | flops 2048 | bytes 16384 | tf_op jit(solution)/shard_map/pmax | solution.py:24
  138.3 3.1 exponential_reduce_fusion.4
  141.4 56.7 %psum.57 = f32[2048]{0:T(1024)S(1)} all-reduce(f32[2048]{0:T(1024)S(1)} %exponential_reduce_fusion.4), channel_id=1, replica_groups=mesh['dp'=16,'cent'=32] {'cent'}, use_global_device_ids=true, to_apply=%region_9.0 | all-reduce | flops 2048 | bytes 16384 | tf_op jit(solution)/shard_map/psum | solution.py:25
  198.1 2.7 fusion.2
  200.8 51.4 %pmax.44 = f32[512]{0:T(512)S(1)} all-reduce(f32[512]{0:T(512)S(1)} %fusion.2), channel_id=1, replica_groups=mesh['dp'=16,'cent'=32] {'dp'}, use_global_device_ids=true, to_apply=%region_11.0 | all-reduce | flops 512 | bytes 4096 | tf_op jit(solution)/shard_map/pmax | solution.py:30
  252.2 3.1 exponential_reduce_fusion.3
  255.4 23.5 %psum.58 = f32[512]{0:T(512)S(1)} all-reduce(f32[512]{0:T(512)S(1)} %exponential_reduce_fusion.3), channel_id=1, replica_groups=mesh['dp'=16,'cent'=32] {'dp'}, use_global_device_ids=true, to_apply=%region_13.0 | all-reduce | flops 512 | bytes 4096 | tf_op jit(solution)/shard_map/psum | solution.py:31
  278.9 2.7 fusion.3
  281.6 59.1 %pmax.45 = f32[2048]{0:T(1024)S(1)} all-reduce(f32[2048]{0:T(1024)S(1)} %fusion.3), channel_id=1, replica_groups=mesh['dp'=16,'cent'=32] {'cent'}, use_global_device_ids=true, to_apply=%region_15.0 | all-reduce | flops 2048 | bytes 16384 | tf_op jit(solution)/shard_map/pmax | solution.py:24
  340.7 3.1 exponential_reduce_fusion.2
  343.8 57.1 %psum.59 = f32[2048]{0:T(1024)S(1)} all-reduce(f32[2048]{0:T(1024)S(1)} %exponential_reduce_fusion.2), channel_id=1, replica_groups=mesh['dp'=16,'cent'=32] {'cent'}, use_global_device_ids=true, to_apply=%region_17.0 | all-reduce | flops 2048 | bytes 16384 | tf_op jit(solution)/shard_map/psum | solution.py:25
  400.9 2.7 fusion.4
  403.6 50.7 %pmax.46 = f32[512]{0:T(512)S(1)} all-reduce(f32[512]{0:T(512)S(1)} %fusion.4), channel_id=1, replica_groups=mesh['dp'=16,'cent'=32] {'dp'}, use_global_device_ids=true, to_apply=%region_19.0 | all-reduce | flops 512 | bytes 4096 | tf_op jit(solution)/shard_map/pmax | solution.py:30
  454.3 3.1 exponential_reduce_fusion.1
  457.4 23.5 %psum.60 = f32[512]{0:T(512)S(1)} all-reduce(f32[512]{0:T(512)S(1)} %exponential_reduce_fusion.1), channel_id=1, replica_groups=mesh['dp'=16,'cent'=32] {'dp'}, use_global_device_ids=true, to_apply=%region_21.0 | all-reduce | flops 512 | bytes 4096 | tf_op jit(solution)/shard_map/psum | solution.py:31
  481.0 0.0 copy-start
  481.0 2.7 fusion.5
  483.7 59.2 %pmax.47 = f32[2048]{0:T(1024)S(1)} all-reduce(f32[2048]{0:T(1024)S(1)} %fusion.5), channel_id=1, replica_groups=mesh['dp'=16,'cent'=32] {'cent'}, use_global_device_ids=true, to_apply=%region_23.0 | all-reduce | flops 2048 | bytes 16384 | tf_op jit(solution)/shard_map/pmax | solution.py:24
  542.9 3.1 exponential_reduce_fusion
  546.0 57.2 %psum.61 = f32[2048]{0:T(1024)S(1)} all-reduce(f32[2048]{0:T(1024)S(1)} %exponential_reduce_fusion), channel_id=1, replica_groups=mesh['dp'=16,'cent'=32] {'cent'}, use_global_device_ids=true, to_apply=%region_25.0 | all-reduce | flops 2048 | bytes 16384 | tf_op jit(solution)/shard_map/psum | solution.py:25
  603.2 0.0 copy-done
  603.2 4.0 fusion.8
  607.2 0.0 all-reduce.2.cloned.1.call-update
  607.3 3.3 fusion.6
  610.6 50.7 %psum.63 = f32[512]{0:T(512)S(1)} all-reduce(f32[512]{0:T(512)S(1)} %fusion.6), channel_id=1, replica_groups=mesh['dp'=16,'cent'=32] {'dp'}, use_global_device_ids=true, to_apply=%region_28.0 | all-reduce | flops 512 | bytes 4096 | tf_op jit(solution)/shard_map/psum | solution.py:83
  661.3 0.6 broadcast_multiply_fusion
  661.9 77.4 %all-reduce.2.cloned.1.call-done = f32[512,128]{1,0:T(8,128)} async-done(((f32[512,128]{1,0:T(8,128)}), f32[512,128]{1,0:T(8,128)}) %all-reduce.2.cloned.1.call-update) | async-done | bytes 262160 | tf_op jit(solution)/shard_map/psum | solution.py:83
  739.3 1.8 broadcast_divide_fusion
  (6 shorter events, 0.1 us)
Async XLA Ops:
  7.2 732.1 %all-reduce.2.cloned.1.call-start = ((), (), s32[]{:S(2)}) async-start(), calls=%async_computation | async-start | bytes 524288 | tf_op jit(solution)/shard_map/psum | solution.py:83
  481.0 122.3 %copy-start = (bf16[2048,128]{1,0:T(8,128)(2,1)S(1)}, bf16[2048,128]{1,0:T(8,128)(2,1)}, u32[]{:S(2)}) copy-start(bf16[2048,128]{1,0:T(8,128)(2,1)} %param.3) | copy-start | bytes 1572868
Sparse Core Ops, SparseCore 0:
  607.4 131.8 all-reduce.1
where the time goes:
time: 749 us; the launch traced here: 748 us
  blocking collectives  608 us (81%)
  waiting for transfers between devices  77.4 us (10%)
  other arithmetic  40.2 us (5%)
  between operations  14.2 us (2%)
  matrix products  8.04 us (1%)
    pmax x3, blocking collectives, source_side_softmaximum(): top = lax.pmax(jnp.max(unnormalized_affinity, axis=1), 'cent')  181 us
    psum x3, blocking collectives, source_side_softmaximum(): lax.psum(jnp.sum(jnp.exp(unnormalized_affinity - top[:, None]), axis=1),...  171 us
    pmax x3, blocking collectives, column_logsumexp(): top = lax.pmax(jnp.max(unnormalized_affinity, axis=0), 'dp')  133 us
    psum x1, waiting for transfers between devices, shards(): numer, mass = lax.psum((numer_part, mass_part), 'dp')  77.4 us
    psum x3, blocking collectives, column_logsumexp(): lax.psum(jnp.sum(jnp.exp(unnormalized_affinity - top[None, :]), axis=0),...  72.9 us
    psum x1, blocking collectives, shards(): numer, mass = lax.psum((numer_part, mass_part), 'dp')  50.7 us
  transfers between devices with their start and end apart: 1, of which 1 were waited for; matrix products, arithmetic and copies ran while one was open for 1% of the time, Pallas kernels for 0%

commit v1 on v0

v1 whole, which is shorter than its diff:
```python
import math

import jax
import jax.numpy as jnp
from jax import lax
from jax.sharding import PartitionSpec as P

LANES = 128


def spread(vector, axis):
    size = lax.axis_size(axis)
    tile = vector.reshape(1, -1, LANES)
    copies = jnp.broadcast_to(tile, (size,) + tile.shape[1:])
    return lax.all_to_all(copies, axis, 0, 0).reshape(size, -1)


def spread_lse(vector, axis):
    parts = spread(vector, axis)
    top = jnp.max(parts, axis=0)
    return top + jnp.log(jnp.sum(jnp.exp(parts - top[None, :]), axis=0))


def spread_sum(vector, axis):
    return jnp.sum(spread(vector, axis), axis=0)


def shards(tokens, centroids, diagonal_factors):
    dp = lax.axis_size("dp")
    tok_local, dim = tokens.shape
    cent_local = centroids.shape[0]
    tok_count = tok_local * dp
    cent_count = cent_local * lax.axis_size("cent")
    ratio = tok_count / cent_count

    cent_float = centroids.astype(jnp.float32)
    scaled = (cent_float * diagonal_factors[None, :]).astype(jnp.bfloat16)
    cent_norm = jnp.sum(cent_float * cent_float * diagonal_factors[None, :], axis=1)
    tok_float = tokens.astype(jnp.float32)
    tok_norm = jnp.sum(tok_float * tok_float * diagonal_factors[None, :], axis=1)
    cross = lax.dot_general(
        scaled, tokens, (((1,), (1,)), ((), ())), preferred_element_type=jnp.float32
    )
    score = 0.5 * cross - 0.25 * tok_norm[None, :] - 0.25 * cent_norm[:, None]

    top = jnp.max(score, axis=1)
    part = top + jnp.log(jnp.sum(jnp.exp(score - top[:, None]), axis=1))
    col = -math.log(cent_count) - spread_lse(part, "dp")
    shifted = score + col[:, None]
    top = jnp.max(shifted, axis=0)
    kept = jnp.exp(shifted - top[None, :])
    part = top + jnp.log(jnp.sum(kept, axis=0))
    gain = jnp.exp(top - spread_lse(part, "cent"))

    weight = gain
    scale = None
    for iteration in range(2):
        mass = spread_sum(jnp.sum(kept * weight[None, :], axis=1), "dp")
        scale = ratio / mass
        rows = spread_sum(gain * jnp.sum(kept * scale[:, None], axis=0), "cent")
        weight = gain / rows

    share = kept * weight[None, :]
    mass_part = scale * jnp.sum(share, axis=1)
    numer_part = scale[:, None] * lax.dot_general(
        share.astype(jnp.bfloat16),
        tokens,
        (((1,), (0,)), ((), ())),
        preferred_element_type=jnp.float32,
    )
    rows = cent_local // dp
    packed = jnp.concatenate(
        [
            numer_part.reshape(dp, rows, dim),
            jnp.pad(mass_part.reshape(dp, 1, rows), ((0, 0), (0, 7), (0, dim - rows))),
        ],
        axis=1,
    )
    total = jnp.sum(lax.all_to_all(packed, "dp", 0, 0), axis=0)
    mass = total[rows, :rows]
    done = jnp.concatenate(
        [
            total[:rows] / mass[:, None],
            jnp.pad((mass / ratio)[None, :], ((0, 7), (0, dim - rows))),
        ],
        axis=0,
    )
    whole = lax.all_to_all(
        jnp.broadcast_to(done[None], (dp,) + done.shape), "dp", 0, 0
    )
    new_centroids = whole[:, :rows].reshape(cent_local, dim)
    masses = whole[:, rows, :rows].reshape(cent_local)
    return (new_centroids, masses)


def solution(mesh):
    return jax.shard_map(
        shards,
        mesh=mesh,
        in_specs=(P("dp", None), P("cent", None), P()),
        out_specs=(P("cent", None), P("cent")),
        check_vma=False,
    )
```

time: 749 us -> 160 us (0.21)
  blocking collectives: 608 us -> 114 us
  waiting for transfers between devices: 77.4 us -> 9.59 us
  other arithmetic: 40.2 us -> 23.1 us
  between operations: 14.2 us -> 0.87 us
    pmax x6 -> x0, blocking collectives: 313 us -> none  [the longest x3 181 us: source_side_softmaximum(): top = lax.pmax(jnp.max(unnormalized_affinity, axis=1), 'cent')]
    psum x7 -> x0, blocking collectives: 295 us -> none  [the longest x3 171 us: source_side_softmaximum(): lax.psum(jnp.sum(jnp.exp(unnormalized_affinity - top[:, None]), axis=1),...]
    all_to_all x0 -> x7, blocking collectives: none -> 114 us  [the longest x5 78.9 us: spread(): return lax.all_to_all(copies, axis, 0, 0).reshape(size, -1)]
    psum x1 -> x0, waiting for transfers between devices: 77.4 us -> none  [shards(): numer, mass = lax.psum((numer_part, mass_part), 'dp')]
    reduce_max x5 -> x3, other arithmetic: 13.4 us -> 2.75 us  [the longest x1 2.69 us: shards(): top = jnp.max(shifted, axis=0)]
    all_to_all x0 -> x1, waiting for transfers between devices: none -> 9.59 us  [spread(): return lax.all_to_all(copies, axis, 0, 0).reshape(size, -1)]
    reduce_sum x8 -> x15, other arithmetic: 23.3 us -> 19 us  [the longest x2 6.31 us: shards(): rows = spread_sum(gain * jnp.sum(kept * scale[:, None], axis=0), 'cent')]
  transfers between devices with their start and end apart: 1 -> 1, of which waited for: 1 -> 1; matrix products, arithmetic and copies ran while one was open for 1% -> 0% of each run, Pallas kernels for 0% -> 0%
where the time goes in v1:
time: 160 us
  blocking collectives  114 us (71%)
  other arithmetic  23.1 us (14%)
  waiting for transfers between devices  9.59 us (6%)
  local copies, waits for them, and re-layouts  5.13 us (3%)
  starting transfers between devices  4.14 us (3%)
  matrix products  2.96 us (2%)
    all_to_all x5, blocking collectives, spread(): return lax.all_to_all(copies, axis, 0, 0).reshape(size, -1)  78.9 us
    all_to_all x1, blocking collectives, shards(): total = jnp.sum(lax.all_to_all(packed, 'dp', 0, 0), axis=0)  19.2 us
    all_to_all x1, blocking collectives, shards(): lax.all_to_all(jnp.broadcast_to(done[None], (dp,) + done.shape), 'dp', 0, 0)  15.9 us
    all_to_all x1, waiting for transfers between devices, spread(): return lax.all_to_all(copies, axis, 0, 0).reshape(size, -1)  9.59 us
    reduce_sum x2, other arithmetic, shards(): rows = spread_sum(gain * jnp.sum(kept * scale[:, None], axis=0), 'cent')  6.31 us
    reduce_sum x2, other arithmetic, shards(): mass = spread_sum(jnp.sum(kept * weight[None, :], axis=1), 'dp')  6.31 us
    all_to_all x1, starting transfers between devices, spread(): return lax.all_to_all(copies, axis, 0, 0).reshape(size, -1)  4.14 us
    reduce_sum x1, other arithmetic, shards(): mass_part = scale * jnp.sum(share, axis=1)  3.31 us
  transfers between devices with their start and end apart: 1, of which 1 were waited for; matrix products, arithmetic and copies ran while one was open for 0% of the time, Pallas kernels for 0%

profile of v1, /device:TPU:1, one launch (start us, length us, event | category | flops | bytes accessed | tf_op | source)
XLA Modules:
  0.0 159.7 jit_solution(9649071313917808376)
XLA Ops:
  0.6 1.1 fusion.5
  1.7 1.4 multiply_reduce_fusion.5
  3.1 2.0 %fusion.11 = (f32[512]{0:T(512)S(1)}, f32[512,2048]{1,0:T(8,128)S(1)}) fusion(f32[512]{0:T(512)S(1)} %broadcast_multiply_fusion.1, f32[2048]{0:T(1024)S(1)} %broadcast_multiply_fusion, bf16[2048,128]{1,0:T(8,128)(2,1)} %param.3, bf16[512,128]{1,0:T(8,128)(2,1)} %param.4, f32[128]{0:T(128)} %param.5), kind=kOutput, calls=%fused_computation.47 | convolution fusion | flops 272825856 | bytes 4862464 | tf_op jit(solution)/shard_map/dot_general | solution.py:41
  5.1 0.0 copy-start
  5.1 1.9 %copy-done = f32[512,2048]{1,0:T(8,128)} copy-done((f32[512,2048]{1,0:T(8,128)}, f32[512,2048]{1,0:T(8,128)S(1)}, u32[]{:S(2)}) %copy-start) | copy-done | bytes 4194328
  7.0 0.7 exponential_reduce_fusion
  7.7 19.0 %all_to_all.40 = f32[16,4,128]{2,1,0:T(4,128)S(1)} all-to-all(f32[16,4,128]{2,1,0:T(4,128)S(1)} %broadcast_in_dim.18), channel_id=1, replica_groups=mesh['dp'=16,'cent'=32] {'dp'}, dimensions={0} | all-to-all | bytes 65536 | tf_op jit(solution)/shard_map/all_to_all | solution.py:15
  26.8 0.0 copy-start.1
  26.8 2.7 %add_reduce_fusion = f32[2048]{0:T(1024)S(1)} fusion(f32[512,2048]{1,0:T(8,128)} %copy-done, f32[512]{0:T(512)S(1)} %subtract_bitcast_fusion), kind=kLoop, calls=%fused_computation.9 | loop fusion | flops 2095104 | bytes 4204544 | tf_op jit(solution)/shard_map/reduce_max | solution.py:50
  29.5 0.7 copy-done.1
  30.2 0.8 fusion.10
  31.1 19.1 %all_to_all.41 = f32[32,16,128]{2,1,0:T(8,128)S(1)} all-to-all(f32[32,16,128]{2,1,0:T(8,128)S(1)} %broadcast_in_dim.19), channel_id=1, replica_groups=mesh['dp'=16,'cent'=32] {'cent'}, dimensions={0} | all-to-all | bytes 524288 | tf_op jit(solution)/shard_map/all_to_all | solution.py:15
  50.2 0.1 exponential_reduce_fusion.1
  50.3 3.2 %multiply_reduce_fusion.3 = f32[512]{0:T(512)S(1)} fusion(f32[2048]{0:T(1024)S(1)} %fusion.8, f32[2048]{0:T(1024)S(1)} %add_reduce_fusion, f32[512,2048]{1,0:T(8,128)} %copy-done, f32[512]{0:T(512)S(1)} %subtract_bitcast_fusion), kind=kLoop, calls=%fused_computation.3 | loop fusion | flops 4193792 | bytes 4214784 | tf_op jit(solution)/shard_map/reduce_sum | solution.py:58
  53.5 13.6 %all_to_all.42 = f32[16,4,128]{2,1,0:T(4,128)S(1)} all-to-all(f32[16,4,128]{2,1,0:T(4,128)S(1)} %broadcast_in_dim.21), channel_id=1, replica_groups=mesh['dp'=16,'cent'=32] {'dp'}, dimensions={0} | all-to-all | bytes 65536 | tf_op jit(solution)/shard_map/all_to_all | solution.py:15
  67.1 3.1 %multiply_reduce_fusion.2 = f32[2048]{0:T(1024)S(1)} fusion(f32[512]{0:T(512)S(1)} %divide_bitcast_fusion, f32[2048]{0:T(1024)S(1)} %add_reduce_fusion, f32[512,2048]{1,0:T(8,128)} %copy-done, f32[512]{0:T(512)S(1)} %subtract_bitcast_fusion), kind=kLoop, calls=%fused_computation.2 | loop fusion | flops 4192256 | bytes 4214784 | tf_op jit(solution)/shard_map/reduce_sum | solution.py:60
  70.3 13.6 %all_to_all.43 = f32[32,16,128]{2,1,0:T(8,128)S(1)} all-to-all(f32[32,16,128]{2,1,0:T(8,128)S(1)} %broadcast_in_dim.22), channel_id=1, replica_groups=mesh['dp'=16,'cent'=32] {'cent'}, dimensions={0} | all-to-all | bytes 524288 | tf_op jit(solution)/shard_map/all_to_all | solution.py:15
  84.0 3.1 %multiply_reduce_fusion.1 = f32[512]{0:T(512)S(1)} fusion(f32[2048]{0:T(1024)S(1)} %bitcast_divide_fusion.1, f32[2048]{0:T(1024)S(1)} %add_reduce_fusion, f32[512,2048]{1,0:T(8,128)} %copy-done, f32[512]{0:T(512)S(1)} %subtract_bitcast_fusion), kind=kLoop, calls=%fused_computation.1 | loop fusion | flops 4193792 | bytes 4214784 | tf_op jit(solution)/shard_map/reduce_sum | solution.py:58
  87.1 13.6 %all_to_all.44 = f32[16,4,128]{2,1,0:T(4,128)S(1)} all-to-all(f32[16,4,128]{2,1,0:T(4,128)S(1)} %broadcast_in_dim.24), channel_id=1, replica_groups=mesh['dp'=16,'cent'=32] {'dp'}, dimensions={0} | all-to-all | bytes 65536 | tf_op jit(solution)/shard_map/all_to_all | solution.py:15
  100.8 0.0 copy-start.3
  100.8 3.2 %multiply_reduce_fusion = f32[2048]{0:T(1024)S(1)} fusion(f32[512]{0:T(512)S(1)} %fusion.14, f32[2048]{0:T(1024)S(1)} %add_reduce_fusion, f32[512,2048]{1,0:T(8,128)} %copy-done, f32[512]{0:T(512)S(1)} %subtract_bitcast_fusion), kind=kLoop, calls=%fused_computation | loop fusion | flops 4192256 | bytes 4214784 | tf_op jit(solution)/shard_map/reduce_sum | solution.py:60
  104.0 0.7 broadcast_in_dim.25
  104.7 4.1 %all-to-all-start.5 = ((f32[32,16,128]{2,1,0:T(8,128)}), f32[32,16,128]{2,1,0:T(8,128)S(1)}, u32[]{:S(2)}, u32[]{:S(2)}) async-start(f32[32,16,128]{2,1,0:T(8,128)} %broadcast_in_dim.25), calls=%async_computation.5 | async-start | bytes 524288 | tf_op jit(solution)/shard_map/all_to_all | solution.py:15
  108.9 0.1 div.66
  108.9 9.6 %all-to-all-done.5 = f32[32,16,128]{2,1,0:T(8,128)S(1)} async-done(((f32[32,16,128]{2,1,0:T(8,128)}), f32[32,16,128]{2,1,0:T(8,128)S(1)}, u32[]{:S(2)}, u32[]{:S(2)}) %all-to-all-start.5) | async-done | bytes 262176 | tf_op jit(solution)/shard_map/all_to_all | solution.py:15
  118.6 0.0 copy-start.2
  118.6 3.3 %multiply_reduce_fusion.4 = f32[512]{0:T(512)S(1)} fusion(f32[2048]{0:T(1024)S(1)} %bitcast_divide_fusion, f32[2048]{0:T(1024)S(1)} %add_reduce_fusion, f32[512,2048]{1,0:T(8,128)} %copy-done, f32[512]{0:T(512)S(1)} %subtract_bitcast_fusion), kind=kLoop, calls=%fused_computation.7 | loop fusion | flops 4193792 | bytes 4214784 | tf_op jit(solution)/shard_map/reduce_sum | solution.py:64
  121.9 0.0 copy-done.3
  121.9 0.1 copy-done.2
  122.0 1.0 fusion.2
  123.0 0.1 reduce_sum.173
  123.1 19.2 %all_to_all.45 = f32[16,40,128]{2,1,0:T(8,128)S(1)} all-to-all(f32[16,40,128]{2,1,0:T(8,128)S(1)} %select_maximum_fusion), channel_id=1, replica_groups=mesh['dp'=16,'cent'=32] {'dp'}, dimensions={0} | all-to-all | bytes 655360 | tf_op jit(solution)/shard_map/all_to_all | solution.py:79
  142.3 0.1 slice_divide_fusion
  142.5 15.9 %all_to_all.46 = f32[16,40,128]{2,1,0:T(8,128)S(1)} all-to-all(f32[16,40,128]{2,1,0:T(8,128)S(1)} %broadcast_in_dim.26), channel_id=1, replica_groups=mesh['dp'=16,'cent'=32] {'dp'}, dimensions={0} | all-to-all | bytes 655360 | tf_op jit(solution)/shard_map/all_to_all | solution.py:88
  158.4 0.7 reshape_squeeze.3
  159.0 0.7 slice.18
  (32 shorter events, 0.5 us)
Async XLA Ops:
  5.1 1.9 %copy-start = (f32[512,2048]{1,0:T(8,128)}, f32[512,2048]{1,0:T(8,128)S(1)}, u32[]{:S(2)}) copy-start(f32[512,2048]{1,0:T(8,128)S(1)} %get-tuple-element.5) | copy-start | bytes 12582916
  26.8 3.4 %copy-start.1 = (f32[512,2048]{1,0:T(8,128)S(1)}, f32[512,2048]{1,0:T(8,128)}, u32[]{:S(2)}) copy-start(f32[512,2048]{1,0:T(8,128)} %copy-done) | copy-start | bytes 12582916
  100.8 21.1 %copy-start.3 = (bf16[2048,128]{1,0:T(8,128)(2,1)S(1)}, bf16[2048,128]{1,0:T(8,128)(2,1)}, u32[]{:S(2)}) copy-start(bf16[2048,128]{1,0:T(8,128)(2,1)} %param.3) | copy-start | bytes 1572868
  104.7 13.8 %all-to-all-start.5 = ((f32[32,16,128]{2,1,0:T(8,128)}), f32[32,16,128]{2,1,0:T(8,128)S(1)}, u32[]{:S(2)}, u32[]{:S(2)}) async-start(f32[32,16,128]{2,1,0:T(8,128)} %broadcast_in_dim.25), calls=%async_computation.5 | async-start | bytes 524288 | tf_op jit(solution)/shard_map/all_to_all | solution.py:15
  118.6 3.5 %copy-start.2 = (f32[512,2048]{1,0:T(8,128)S(1)}, f32[512,2048]{1,0:T(8,128)}, u32[]{:S(2)}) copy-start(f32[512,2048]{1,0:T(8,128)} %copy-done) | copy-start | bytes 12582916

commit v2 on v1

v2 whole, which is shorter than its diff:
```python
import functools
import math

import jax
import jax.numpy as jnp
from jax import lax
from jax.experimental import pallas as pl
from jax.experimental.pallas import tpu as pltpu
from jax.sharding import PartitionSpec as P

LANES = 128
TILE = 256
F32 = jnp.float32
BF16 = jnp.bfloat16


def along_lanes(a, b):
    return lax.dot_general(a, b, (((1,), (1,)), ((), ())), preferred_element_type=F32)


def plain(a, b):
    return lax.dot_general(a, b, (((1,), (0,)), ((), ())), preferred_element_type=F32)


def combine_lse(parts_ref):
    parts = parts_ref[...]
    top = jnp.max(parts, axis=0)
    return top + jnp.log(jnp.sum(jnp.exp(parts - top[None]), axis=0))


def pair_of_rows(dense, k):
    return jnp.concatenate([dense[2 * k : 2 * k + 1], dense[2 * k + 1 : 2 * k + 2]], axis=1)


def two_terms(vector):
    wide = jnp.broadcast_to(vector, (16, vector.shape[1]))
    high = wide.astype(BF16)
    low = wide - high.astype(F32)
    row = lax.broadcasted_iota(jnp.int32, wide.shape, 0)
    return jnp.where(row == 0, high.astype(F32), jnp.where(row == 1, low, 0.0)).astype(BF16)


def dense_rows(vector):
    count = vector.shape[1] // LANES
    return jnp.concatenate(
        [vector[:, k * LANES : (k + 1) * LANES] for k in range(count)], axis=0
    )


def column_sums(kept_ref, weight):
    total = None
    for k in range(kept_ref.shape[1] // TILE):
        term = along_lanes(
            two_terms(pair_of_rows(weight, k)), kept_ref[:, k * TILE : (k + 1) * TILE]
        )
        total = term if total is None else total + term
    return dense_rows(jnp.sum(total, axis=0, keepdims=True))


def row_sums(kept_ref, scale):
    total = None
    for k in range(kept_ref.shape[0] // TILE):
        term = plain(two_terms(pair_of_rows(scale, k)), kept_ref[k * TILE : (k + 1) * TILE, :])
        total = term if total is None else total + term
    return dense_rows(jnp.sum(total, axis=0, keepdims=True))


def spread_out(out_ref, dense):
    out_ref[...] = jnp.broadcast_to(dense[None], out_ref.shape)


def first_columns(tok_ref, cent_ref, diag_ref, out_ref, half_ref):
    diag = diag_ref[...]
    half = (0.5 * (cent_ref[...].astype(F32) * diag).astype(BF16).astype(F32)).astype(BF16)
    half_ref[...] = half
    top = total = None
    for k in range(tok_ref.shape[0] // TILE):
        tok = tok_ref[k * TILE : (k + 1) * TILE, :]
        wide = tok.astype(F32)
        norm = 0.25 * jnp.sum(wide * wide * diag, axis=1, keepdims=True)
        score = along_lanes(tok, half) - norm
        here = jnp.max(score, axis=0, keepdims=True)
        new = here if top is None else jnp.maximum(top, here)
        part = jnp.sum(jnp.exp(score - new), axis=0, keepdims=True)
        total = part if top is None else total * jnp.exp(top - new) + part
        top = new
    spread_out(out_ref, dense_rows(top + jnp.log(total)))


def first_rows(cent_count, parts_ref, tok_ref, half_ref, norm_ref, kept_ref, top_ref, out_ref, sum_ref):
    norm = norm_ref[...]
    col = (-math.log(cent_count) - (combine_lse(parts_ref) - norm)) - norm
    column = jnp.concatenate(
        [jnp.broadcast_to(col[k : k + 1], (LANES, LANES)).T for k in range(col.shape[0])], axis=0
    )
    column = jnp.concatenate([column] * (TILE // LANES), axis=1)
    half = half_ref[...]
    for k in range(tok_ref.shape[0] // TILE):
        score = along_lanes(half, tok_ref[k * TILE : (k + 1) * TILE, :]) + column
        top = jnp.max(score, axis=0, keepdims=True)
        kept = jnp.exp(score - top)
        kept_ref[:, k * TILE : (k + 1) * TILE] = kept.astype(BF16)
        total = top + jnp.log(jnp.sum(kept, axis=0, keepdims=True))
        for h in range(TILE // LANES):
            at = k * (TILE // LANES) + h
            top_ref[at : at + 1, :] = top[:, h * LANES : (h + 1) * LANES]
            sum_ref[at : at + 1, :] = total[:, h * LANES : (h + 1) * LANES]
    spread_out(out_ref, sum_ref[...])


def second_columns(parts_ref, top_ref, norm_ref, kept_ref, out_ref, gain_ref):
    norm = norm_ref[...]
    gain = jnp.exp((top_ref[...] - norm) - (combine_lse(parts_ref) - norm))
    gain_ref[...] = gain
    spread_out(out_ref, column_sums(kept_ref, gain))


def later_rows(ratio, parts_ref, gain_ref, kept_ref, out_ref, scale_ref):
    scale = ratio / jnp.sum(parts_ref[...], axis=0)
    scale_ref[...] = scale
    spread_out(out_ref, gain_ref[...] * row_sums(kept_ref, scale))


def later_columns(parts_ref, gain_ref, kept_ref, out_ref):
    weight = gain_ref[...] / jnp.sum(parts_ref[...], axis=0)
    spread_out(out_ref, column_sums(kept_ref, weight))


def numerators(rows, parts_ref, gain_ref, kept_ref, tok_ref, out_ref):
    weight = gain_ref[...] / jnp.sum(parts_ref[...], axis=0)
    ones = jnp.ones((TILE, LANES), BF16)
    total = None
    for k in range(kept_ref.shape[1] // TILE):
        at = slice(k * TILE, (k + 1) * TILE)
        share = (kept_ref[:, at].astype(F32) * pair_of_rows(weight, k)).astype(BF16)
        term = plain(share, jnp.concatenate([tok_ref[at, :], ones], axis=1))
        total = term if total is None else total + term
    chunks = out_ref.shape[0]
    out_ref[:, :rows, :] = total[:, :LANES].reshape(chunks, rows, LANES)
    per = LANES // rows
    for g in range(total.shape[0] // LANES):
        mass = total[g * LANES : (g + 1) * LANES, LANES:].T[:8]
        for q in range(per):
            turned = mass if q == 0 else pltpu.roll(mass, LANES - q * rows, 1)
            out_ref[g * per + q, rows:, :] = turned


def divide(rows, parts_ref, out_ref):
    total = jnp.sum(parts_ref[...], axis=0)
    mass = jnp.broadcast_to(total[rows : rows + 1], (LANES, LANES)).T[:rows]
    out_ref[:, :rows, :] = jnp.broadcast_to(
        (total[:rows] / mass)[None], (out_ref.shape[0], rows, LANES)
    )
    out_ref[:, rows:, :] = jnp.broadcast_to(total[rows:][None], (out_ref.shape[0], 8, LANES))


def unpack(rows, ratio, parts_ref, scale_ref, cent_ref, mass_ref):
    cent_ref[...] = parts_ref[:, :rows, :].reshape(cent_ref.shape)
    per = LANES // rows
    lane = lax.broadcasted_iota(jnp.int32, (8, LANES), 1)
    for g in range(mass_ref.shape[0]):
        mass = parts_ref[g * per, rows:, :]
        for q in range(1, per):
            turned = pltpu.roll(parts_ref[g * per + q, rows:, :], q * rows, 1)
            mass = jnp.where(lane >= q * rows, turned, mass)
        mass_ref[g : g + 1, :] = mass[:1] * scale_ref[g : g + 1, :] / ratio


def run(kernel, outs, *operands, scratch=()):
    vmem = pl.BlockSpec(memory_space=pltpu.VMEM)
    return pl.pallas_call(
        kernel,
        out_shape=[jax.ShapeDtypeStruct(shape, kind) for shape, kind in outs],
        in_specs=[vmem] * len(operands),
        out_specs=[vmem] * len(outs),
        scratch_shapes=list(scratch),
        compiler_params=pltpu.CompilerParams(vmem_limit_bytes=24 * 1024 * 1024),
    )(*operands)


def shards(tokens, centroids, diagonal_factors):
    dp, cent = lax.axis_size("dp"), lax.axis_size("cent")
    tok_local, dim = tokens.shape
    cent_local = centroids.shape[0]
    cent_count = cent_local * cent
    ratio = tok_local * dp / cent_count
    rows = cent_local // dp
    by_tok, by_cent = (tok_local // LANES, LANES), (cent_local // LANES, LANES)
    to_dp, to_cent = (dp,) + by_cent, (cent,) + by_tok

    def quarter_norm(vectors):
        wide = vectors.astype(F32)
        return 0.25 * jnp.sum(wide * wide * diagonal_factors[None, :], axis=1)

    def over(axis, copies):
        return lax.all_to_all(copies, axis, 0, 0)

    tok_norm = quarter_norm(tokens).reshape(by_tok)
    cent_norm = quarter_norm(centroids).reshape(by_cent)

    copies, half = run(
        first_columns,
        [(to_dp, F32), ((cent_local, dim), BF16)],
        tokens,
        centroids,
        diagonal_factors.reshape(1, dim),
    )
    kept, top, copies = run(
        functools.partial(first_rows, cent_count),
        [((cent_local, tok_local), BF16), (by_tok, F32), (to_cent, F32)],
        over("dp", copies),
        tokens,
        half,
        cent_norm,
        scratch=[pltpu.VMEM(by_tok, F32)],
    )
    copies, gain = run(
        second_columns,
        [(to_dp, F32), (by_tok, F32)],
        over("cent", copies),
        top,
        tok_norm,
        kept,
    )
    rows_of = functools.partial(later_rows, ratio)
    rows_outs = [(to_cent, F32), (by_cent, F32)]
    copies, scale = run(rows_of, rows_outs, over("dp", copies), gain, kept)
    (copies,) = run(later_columns, [(to_dp, F32)], over("cent", copies), gain, kept)
    copies, scale = run(rows_of, rows_outs, over("dp", copies), gain, kept)

    packed = (dp, rows + 8, LANES)
    (copies,) = run(
        functools.partial(numerators, rows),
        [(packed, F32)],
        over("cent", copies),
        gain,
        kept,
        tokens,
    )
    (copies,) = run(functools.partial(divide, rows), [(packed, F32)], over("dp", copies))
    new_centroids, masses = run(
        functools.partial(unpack, rows, ratio),
        [((cent_local, dim), F32), (by_cent, F32)],
        over("dp", copies),
        scale,
    )
    return (new_centroids, masses.reshape(cent_local))


def solution(mesh):
    return jax.shard_map(
        shards,
        mesh=mesh,
        in_specs=(P("dp", None), P("cent", None), P()),
        out_specs=(P("cent", None), P("cent")),
        check_vma=False,
    )
```

time: 160 us -> 141 us (0.88)
  blocking collectives: 114 us -> 89.4 us
  other arithmetic: 23.1 us -> 2.06 us
  starting transfers between devices: 4.14 us -> 21.5 us
  Pallas kernels: 0 us -> 8.55 us
  waiting for transfers between devices: 9.59 us -> 15 us
  matrix products: 2.96 us -> 0 us
    all_to_all x7 -> x6, blocking collectives: 114 us -> 89.4 us  [over(): return lax.all_to_all(copies, axis, 0, 0)]
    reduce_sum x16 -> x2, other arithmetic: 20.1 us -> 2.05 us  [quarter_norm(): return 0.25 * jnp.sum(wide * wide * diagonal_factors[None, :], axis=1)]
    all_to_all x1 -> x2, starting transfers between devices: 4.14 us -> 21.5 us  [over(): return lax.all_to_all(copies, axis, 0, 0)]
    pallas_call x0 -> x9, Pallas kernels: none -> 8.55 us  [run(): pl.pallas_call(kernel, out_shape=[jax.ShapeDtypeStruct(shape, kind) for s...]
    all_to_all x1 -> x2, waiting for transfers between devices: 9.59 us -> 15 us  [over(): return lax.all_to_all(copies, axis, 0, 0)]
    dot_general x2 -> x0, matrix products: 2.96 us -> none  [the longest x1 1.98 us: shards(): lax.dot_general(scaled, tokens, (((1,), (1,)), ((), ())), preferred_eleme...]
    reduce_max x3 -> x0, other arithmetic: 2.75 us -> none  [the longest x1 2.69 us: shards(): top = jnp.max(shifted, axis=0)]
    unnamed x8 -> x10, local copies, waits for them, and re-layouts: 2.74 us -> 3.64 us
  transfers between devices with their start and end apart: 1 -> 2, of which waited for: 1 -> 2; matrix products, arithmetic and copies ran while one was open for 0% -> 1% of each run, Pallas kernels for 0% -> 0%
where the time goes in v2:
time: 141 us
  blocking collectives  89.4 us (63%)
  starting transfers between devices  21.5 us (15%)
  waiting for transfers between devices  15 us (11%)
  Pallas kernels  8.55 us (6%)
  local copies, waits for them, and re-layouts  3.64 us (3%)
  other arithmetic  2.06 us (1%)
    all_to_all x6, blocking collectives, over(): return lax.all_to_all(copies, axis, 0, 0)  89.4 us
    all_to_all x2, starting transfers between devices, over(): return lax.all_to_all(copies, axis, 0, 0)  21.5 us
    all_to_all x2, waiting for transfers between devices, over(): return lax.all_to_all(copies, axis, 0, 0)  15 us
    pallas_call x9, Pallas kernels, run(): pl.pallas_call(kernel, out_shape=[jax.ShapeDtypeStruct(shape, kind) for s...  8.55 us
    unnamed x10, local copies, waits for them, and re-layouts  3.64 us
  transfers between devices with their start and end apart: 2, of which 2 were waited for; matrix products, arithmetic and copies ran while one was open for 1% of the time, Pallas kernels for 0%

profile of v2, /device:TPU:1, one launch (start us, length us, event | category | flops | bytes accessed | tf_op | source)
XLA Modules:
  0.0 140.9 jit_solution(11508792871541636464)
XLA Ops:
  0.6 0.0 copy-start
  0.6 1.0 copy-done
  1.7 0.0 copy-start.3
  1.7 0.9 copy-done.3
  2.6 0.0 copy-start.4
  2.6 0.7 copy-done.4
  3.2 0.0 copy-start.2
  3.2 2.2 %shard_map.50 = (f32[16,4,128]{2,1,0:T(4,128)}, bf16[512,128]{1,0:T(8,128)(2,1)S(1)}) custom-call(bf16[2048,128]{1,0:T(8,128)(2,1)S(1)} %copy-done, bf16[512,128]{1,0:T(8,128)(2,1)S(1)} %copy-done.3, f32[1,128]{1,0:T(1,128)S(1)} %bitcast.6), custom_call_target="tpu_custom_call" | custom-call | tf_op jit(solution)/shard_map/pallas_call | solution.py:171
  5.4 11.8 %all-to-all-start = ((f32[16,4,128]{2,1,0:T(4,128)}), f32[16,4,128]{2,1,0:T(4,128)S(1)}, u32[]{:S(2)}, u32[]{:S(2)}) async-start(f32[16,4,128]{2,1,0:T(4,128)} %get-tuple-element.14), calls=%async_computation | async-start | bytes 65536 | tf_op jit(solution)/shard_map/all_to_all | solution.py:196
  17.2 1.1 multiply_reduce_fusion.1
  18.3 6.3 %all-to-all-done.parts_ref = f32[16,4,128]{2,1,0:T(4,128)S(1)} async-done(((f32[16,4,128]{2,1,0:T(4,128)}), f32[16,4,128]{2,1,0:T(4,128)S(1)}, u32[]{:S(2)}, u32[]{:S(2)}) %all-to-all-start) | async-done | bytes 32800 | tf_op jit(solution)/shard_map/all_to_all | solution.py:196
  24.6 0.0 copy-start.1
  24.6 1.0 copy-done.1
  25.7 2.3 %shard_map.51 = (bf16[512,2048]{1,0:T(8,128)(2,1)S(1)}, f32[16,128]{1,0:T(8,128)S(1)}, f32[32,16,128]{2,1,0:T(8,128)}) custom-call(f32[16,4,128]{2,1,0:T(4,128)S(1)} %all-to-all-done.parts_ref, bf16[2048,128]{1,0:T(8,128)(2,1)S(1)} %copy-done.1, bf16[512,128]{1,0:T(8,128)(2,1)S(1)} %get-tuple-element.15.half_ref, f32[4,128]{1,0:T(4,128)S(1)} %multiply_bitcast_fusion.1.norm_ref), custom_call_target="tpu_custom_call" | custom-call | tf_op jit(solution)/shard_map/pallas_call | solution.py:171
  28.0 9.7 %all-to-all-start.1 = ((f32[32,16,128]{2,1,0:T(8,128)}), f32[32,16,128]{2,1,0:T(8,128)S(1)}, u32[]{:S(2)}, u32[]{:S(2)}) async-start(f32[32,16,128]{2,1,0:T(8,128)} %get-tuple-element.16), calls=%async_computation.1 | async-start | bytes 524288 | tf_op jit(solution)/shard_map/all_to_all | solution.py:196
  37.7 0.0 copy-done.2
  37.7 1.0 multiply_reduce_fusion
  38.7 8.6 %all-to-all-done.1.parts_ref = f32[32,16,128]{2,1,0:T(8,128)S(1)} async-done(((f32[32,16,128]{2,1,0:T(8,128)}), f32[32,16,128]{2,1,0:T(8,128)S(1)}, u32[]{:S(2)}, u32[]{:S(2)}) %all-to-all-start.1) | async-done | bytes 262176 | tf_op jit(solution)/shard_map/all_to_all | solution.py:196
  47.4 0.7 shard_map.52
  48.1 13.6 %all_to_all.40.parts_ref = f32[16,4,128]{2,1,0:T(4,128)S(1)} all-to-all(f32[16,4,128]{2,1,0:T(4,128)S(1)} %get-tuple-element.19), channel_id=1, replica_groups=mesh['dp'=16,'cent'=32] {'dp'}, dimensions={0} | all-to-all | bytes 65536 | tf_op jit(solution)/shard_map/all_to_all | solution.py:196
  61.6 0.6 shard_map.53
  62.3 13.6 %all_to_all.41.parts_ref = f32[32,16,128]{2,1,0:T(8,128)S(1)} all-to-all(f32[32,16,128]{2,1,0:T(8,128)S(1)} %get-tuple-element.21), channel_id=1, replica_groups=mesh['dp'=16,'cent'=32] {'cent'}, dimensions={0} | all-to-all | bytes 524288 | tf_op jit(solution)/shard_map/all_to_all | solution.py:196
  75.9 0.7 shard_map.54
  76.5 13.6 %all_to_all.42.parts_ref = f32[16,4,128]{2,1,0:T(4,128)S(1)} all-to-all(f32[16,4,128]{2,1,0:T(4,128)S(1)} %shard_map.54), channel_id=1, replica_groups=mesh['dp'=16,'cent'=32] {'dp'}, dimensions={0} | all-to-all | bytes 65536 | tf_op jit(solution)/shard_map/all_to_all | solution.py:196
  90.1 0.4 shard_map.55
  90.5 13.6 %all_to_all.43.parts_ref = f32[32,16,128]{2,1,0:T(8,128)S(1)} all-to-all(f32[32,16,128]{2,1,0:T(8,128)S(1)} %get-tuple-element.22), channel_id=1, replica_groups=mesh['dp'=16,'cent'=32] {'cent'}, dimensions={0} | all-to-all | bytes 524288 | tf_op jit(solution)/shard_map/all_to_all | solution.py:196
  104.1 0.8 shard_map.56
  105.0 19.2 %all_to_all.44.parts_ref = f32[16,40,128]{2,1,0:T(8,128)S(1)} all-to-all(f32[16,40,128]{2,1,0:T(8,128)S(1)} %shard_map.56), channel_id=1, replica_groups=mesh['dp'=16,'cent'=32] {'dp'}, dimensions={0} | all-to-all | bytes 655360 | tf_op jit(solution)/shard_map/all_to_all | solution.py:196
  124.2 0.1 shard_map.57
  124.3 15.9 %all_to_all.45.parts_ref = f32[16,40,128]{2,1,0:T(8,128)S(1)} all-to-all(f32[16,40,128]{2,1,0:T(8,128)S(1)} %shard_map.57), channel_id=1, replica_groups=mesh['dp'=16,'cent'=32] {'dp'}, dimensions={0} | all-to-all | bytes 655360 | tf_op jit(solution)/shard_map/all_to_all | solution.py:196
  140.1 0.7 shard_map.58
  (2 shorter events, 0.0 us)
Async XLA Ops:
  0.6 1.0 copy-start
  1.7 0.9 copy-start.3
  2.6 0.7 copy-start.4
  3.2 34.4 %copy-start.2 = (bf16[2048,128]{1,0:T(8,128)(2,1)S(1)}, bf16[2048,128]{1,0:T(8,128)(2,1)}, u32[]{:S(2)}) copy-start(bf16[2048,128]{1,0:T(8,128)(2,1)} %tok_ref.5) | copy-start | bytes 1572868
  5.4 19.2 %all-to-all-start = ((f32[16,4,128]{2,1,0:T(4,128)}), f32[16,4,128]{2,1,0:T(4,128)S(1)}, u32[]{:S(2)}, u32[]{:S(2)}) async-start(f32[16,4,128]{2,1,0:T(4,128)} %get-tuple-element.14), calls=%async_computation | async-start | bytes 65536 | tf_op jit(solution)/shard_map/all_to_all | solution.py:196
  24.6 1.0 copy-start.1
  28.0 19.4 %all-to-all-start.1 = ((f32[32,16,128]{2,1,0:T(8,128)}), f32[32,16,128]{2,1,0:T(8,128)S(1)}, u32[]{:S(2)}, u32[]{:S(2)}) async-start(f32[32,16,128]{2,1,0:T(8,128)} %get-tuple-element.16), calls=%async_computation.1 | async-start | bytes 524288 | tf_op jit(solution)/shard_map/all_to_all | solution.py:196

commit v3 on v2

--- a/solution.py
+++ b/solution.py
@@ -69,12 +69,25 @@
     out_ref[...] = jnp.broadcast_to(dense[None], out_ref.shape)
 
 
-def first_columns(tok_ref, cent_ref, diag_ref, out_ref, half_ref):
+def first_columns(tok_hbm, cent_hbm, diag_hbm, out_ref, half_ref, tok_ref, cent_ref, diag_ref, sems):
+    loads = [
+        pltpu.make_async_copy(cent_hbm, cent_ref, sems.at[0]),
+        pltpu.make_async_copy(diag_hbm, diag_ref, sems.at[1]),
+    ]
+    tiles = []
+    for k in range(tok_ref.shape[0] // TILE):
+        at = pl.ds(k * TILE, TILE)
+        tiles.append(pltpu.make_async_copy(tok_hbm.at[at], tok_ref.at[at], sems.at[2 + k]))
+    for load in loads + tiles:
+        load.start()
+    for load in loads:
+        load.wait()
     diag = diag_ref[...]
     half = (0.5 * (cent_ref[...].astype(F32) * diag).astype(BF16).astype(F32)).astype(BF16)
     half_ref[...] = half
     top = total = None
-    for k in range(tok_ref.shape[0] // TILE):
+    for k, load in enumerate(tiles):
+        load.wait()
         tok = tok_ref[k * TILE : (k + 1) * TILE, :]
         wide = tok.astype(F32)
         norm = 0.25 * jnp.sum(wide * wide * diag, axis=1, keepdims=True)
@@ -87,7 +100,23 @@
     spread_out(out_ref, dense_rows(top + jnp.log(total)))
 
 
-def first_rows(cent_count, parts_ref, tok_ref, half_ref, norm_ref, kept_ref, top_ref, out_ref, sum_ref):
+def dense_norms(vectors_ref, diag, out_ref):
+    for k in range(out_ref.shape[0]):
+        wide = vectors_ref[k * LANES : (k + 1) * LANES, :].astype(F32)
+        norm = 0.25 * jnp.sum(wide * wide * diag, axis=1, keepdims=True)
+        out_ref[k : k + 1, :] = jnp.broadcast_to(norm, (LANES, LANES)).T[:1]
+
+
+def prepare(tok_ref, cent_ref, diag_ref, half_ref, near_ref, near_half_ref, tok_norm_ref, cent_norm_ref):
+    near_ref[...] = tok_ref[...]
+    near_half_ref[...] = half_ref[...]
+    dense_norms(tok_ref, diag_ref[...], tok_norm_ref)
+    dense_norms(cent_ref, diag_ref[...], cent_norm_ref)
+
+
+def first_rows(
+    cent_count, parts_ref, tok_ref, half_ref, norm_ref, tok_norm_ref, kept_ref, top_ref, out_ref, sum_ref
+):
     norm = norm_ref[...]
     col = (-math.log(cent_count) - (combine_lse(parts_ref) - norm)) - norm
     column = jnp.concatenate(
@@ -105,12 +134,12 @@
             at = k * (TILE // LANES) + h
             top_ref[at : at + 1, :] = top[:, h * LANES : (h + 1) * LANES]
             sum_ref[at : at + 1, :] = total[:, h * LANES : (h + 1) * LANES]
-    spread_out(out_ref, sum_ref[...])
-
-
-def second_columns(parts_ref, top_ref, norm_ref, kept_ref, out_ref, gain_ref):
-    norm = norm_ref[...]
-    gain = jnp.exp((top_ref[...] - norm) - (combine_lse(parts_ref) - norm))
+    top_ref[...] = top_ref[...] - tok_norm_ref[...]
+    spread_out(out_ref, sum_ref[...] - tok_norm_ref[...])
+
+
+def second_columns(parts_ref, top_ref, kept_ref, out_ref, gain_ref):
+    gain = jnp.exp(top_ref[...] - combine_lse(parts_ref))
     gain_ref[...] = gain
     spread_out(out_ref, column_sums(kept_ref, gain))
 
@@ -137,44 +166,35 @@
         total = term if total is None else total + term
     chunks = out_ref.shape[0]
     out_ref[:, :rows, :] = total[:, :LANES].reshape(chunks, rows, LANES)
-    per = LANES // rows
-    for g in range(total.shape[0] // LANES):
-        mass = total[g * LANES : (g + 1) * LANES, LANES:].T[:8]
-        for q in range(per):
-            turned = mass if q == 0 else pltpu.roll(mass, LANES - q * rows, 1)
-            out_ref[g * per + q, rows:, :] = turned
-
-
-def divide(rows, parts_ref, out_ref):
+    groups, per = total.shape[0] // LANES, LANES // rows
+    mass = [total[g * LANES : (g + 1) * LANES, LANES:].T[:1] for g in range(groups)]
+    for k in range(chunks):
+        own = jnp.broadcast_to(mass[k // per], (8, LANES))
+        if k % per:
+            own = pltpu.roll(own, LANES - (k % per) * rows, 1)
+        out_ref[k, rows:, :] = jnp.concatenate(mass + [own[: 8 - groups]], axis=0)
+
+
+def divide(rows, ratio, parts_ref, scale_ref, out_ref, mass_ref):
     total = jnp.sum(parts_ref[...], axis=0)
-    mass = jnp.broadcast_to(total[rows : rows + 1], (LANES, LANES)).T[:rows]
-    out_ref[:, :rows, :] = jnp.broadcast_to(
-        (total[:rows] / mass)[None], (out_ref.shape[0], rows, LANES)
-    )
-    out_ref[:, rows:, :] = jnp.broadcast_to(total[rows:][None], (out_ref.shape[0], 8, LANES))
-
-
-def unpack(rows, ratio, parts_ref, scale_ref, cent_ref, mass_ref):
-    cent_ref[...] = parts_ref[:, :rows, :].reshape(cent_ref.shape)
-    per = LANES // rows
-    lane = lax.broadcasted_iota(jnp.int32, (8, LANES), 1)
-    for g in range(mass_ref.shape[0]):
-        mass = parts_ref[g * per, rows:, :]
-        for q in range(1, per):
-            turned = pltpu.roll(parts_ref[g * per + q, rows:, :], q * rows, 1)
-            mass = jnp.where(lane >= q * rows, turned, mass)
-        mass_ref[g : g + 1, :] = mass[:1] * scale_ref[g : g + 1, :] / ratio
-
-
-def run(kernel, outs, *operands, scratch=()):
-    vmem = pl.BlockSpec(memory_space=pltpu.VMEM)
+    groups = mass_ref.shape[0]
+    mass_ref[...] = total[rows : rows + groups] * scale_ref[...] / ratio
+    own = total[rows + groups : rows + groups + 1]
+    own = jnp.broadcast_to(own, (LANES, LANES)).T[:rows]
+    spread_out(out_ref, total[:rows] / own)
+
+
+def run(kernel, outs, *operands, scratch=(), place=pltpu.VMEM, room=24, cost=0):
     return pl.pallas_call(
         kernel,
         out_shape=[jax.ShapeDtypeStruct(shape, kind) for shape, kind in outs],
-        in_specs=[vmem] * len(operands),
-        out_specs=[vmem] * len(outs),
+        in_specs=[pl.BlockSpec(memory_space=place)] * len(operands),
+        out_specs=[pl.BlockSpec(memory_space=pltpu.VMEM)] * len(outs),
         scratch_shapes=list(scratch),
-        compiler_params=pltpu.CompilerParams(vmem_limit_bytes=24 * 1024 * 1024),
+        cost_estimate=pl.CostEstimate(flops=cost, bytes_accessed=cost, transcendentals=0)
+        if cost
+        else None,
+        compiler_params=pltpu.CompilerParams(vmem_limit_bytes=room * 1024 * 1024),
     )(*operands)
 
 
@@ -188,30 +208,42 @@
     by_tok, by_cent = (tok_local // LANES, LANES), (cent_local // LANES, LANES)
     to_dp, to_cent = (dp,) + by_cent, (cent,) + by_tok
 
-    def quarter_norm(vectors):
-        wide = vectors.astype(F32)
-        return 0.25 * jnp.sum(wide * wide * diagonal_factors[None, :], axis=1)
-
     def over(axis, copies):
         return lax.all_to_all(copies, axis, 0, 0)
 
-    tok_norm = quarter_norm(tokens).reshape(by_tok)
-    cent_norm = quarter_norm(centroids).reshape(by_cent)
-
+    diag = diagonal_factors.reshape(1, dim)
     copies, half = run(
         first_columns,
         [(to_dp, F32), ((cent_local, dim), BF16)],
         tokens,
         centroids,
-        diagonal_factors.reshape(1, dim),
+        diag,
+        scratch=[
+            pltpu.VMEM((tok_local, dim), BF16),
+            pltpu.VMEM((cent_local, dim), BF16),
+            pltpu.VMEM((1, dim), F32),
+            pltpu.SemaphoreType.DMA((2 + tok_local // TILE,)),
+        ],
+        place=pltpu.HBM,
+        room=60,
+    )
+    near, near_half, tok_norm, cent_norm = run(
+        prepare,
+        [((tok_local, dim), BF16), ((cent_local, dim), BF16), (by_tok, F32), (by_cent, F32)],
+        tokens,
+        centroids,
+        diag,
+        half,
+        cost=4 * (tok_local + cent_local) * dim,
     )
     kept, top, copies = run(
         functools.partial(first_rows, cent_count),
         [((cent_local, tok_local), BF16), (by_tok, F32), (to_cent, F32)],
         over("dp", copies),
-        tokens,
-        half,
+        near,
+        near_half,
         cent_norm,
+        tok_norm,
         scratch=[pltpu.VMEM(by_tok, F32)],
     )
     copies, gain = run(
@@ -219,7 +251,6 @@
         [(to_dp, F32), (by_tok, F32)],
         over("cent", copies),
         top,
-        tok_norm,
         kept,
     )
     rows_of = functools.partial(later_rows, ratio)
@@ -235,15 +266,15 @@
         over("cent", copies),
         gain,
         kept,
-        tokens,
-    )
-    (copies,) = run(functools.partial(divide, rows), [(packed, F32)], over("dp", copies))
-    new_centroids, masses = run(
-        functools.partial(unpack, rows, ratio),
-        [((cent_local, dim), F32), (by_cent, F32)],
+        near,
+    )
+    copies, masses = run(
+        functools.partial(divide, rows, ratio),
+        [((dp, rows, dim), F32), (by_cent, F32)],
         over("dp", copies),
         scale,
     )
+    new_centroids = over("dp", copies).reshape(cent_local, dim)
     return (new_centroids, masses.reshape(cent_local))
 
 

time: 141 us -> 139 us (0.986)
  blocking collectives: 89.4 us -> 108 us
  waiting for transfers between devices: 15 us -> 3.08 us
  starting transfers between devices: 21.5 us -> 11.8 us
  Pallas kernels: 8.55 us -> 10.7 us
  other arithmetic: 2.06 us -> 0 us
    all_to_all x6 -> x7, blocking collectives: 89.4 us -> 108 us  [over(): return lax.all_to_all(copies, axis, 0, 0)]
    all_to_all x2 -> x1, waiting for transfers between devices: 15 us -> 3.08 us  [over(): return lax.all_to_all(copies, axis, 0, 0)]
    all_to_all x2 -> x1, starting transfers between devices: 21.5 us -> 11.8 us  [over(): return lax.all_to_all(copies, axis, 0, 0)]
    pallas_call x9, Pallas kernels: 8.55 us -> 10.7 us  [run(): pl.pallas_call(kernel, out_shape=[jax.ShapeDtypeStruct(shape, kind) for s...]
    reduce_sum x2 -> x0, other arithmetic: 2.05 us -> none  [quarter_norm(): return 0.25 * jnp.sum(wide * wide * diagonal_factors[None, :], axis=1)]
    unnamed x10 -> x9, local copies, waits for them, and re-layouts: 3.64 us -> 4.2 us
  transfers between devices with their start and end apart: 2 -> 1, of which waited for: 2 -> 1; matrix products, arithmetic and copies ran while one was open for 1% -> 0% of each run, Pallas kernels for 0% -> 1%
where the time goes in v3:
time: 139 us
  blocking collectives  108 us (78%)
  starting transfers between devices  11.8 us (8%)
  Pallas kernels  10.7 us (8%)
  local copies, waits for them, and re-layouts  4.2 us (3%)
  waiting for transfers between devices  3.08 us (2%)
    all_to_all x7, blocking collectives, over(): return lax.all_to_all(copies, axis, 0, 0)  108 us
    all_to_all x1, starting transfers between devices, over(): return lax.all_to_all(copies, axis, 0, 0)  11.8 us
    pallas_call x9, Pallas kernels, run(): pl.pallas_call(kernel, out_shape=[jax.ShapeDtypeStruct(shape, kind) for s...  10.7 us
    unnamed x9, local copies, waits for them, and re-layouts  4.2 us
    all_to_all x1, waiting for transfers between devices, over(): return lax.all_to_all(copies, axis, 0, 0)  3.08 us
  transfers between devices with their start and end apart: 1, of which 1 were waited for; matrix products, arithmetic and copies ran while one was open for 0% of the time, Pallas kernels for 1%

profile of v3, /device:TPU:1, one launch (start us, length us, event | category | flops | bytes accessed | tf_op | source)
XLA Modules:
  0.0 138.8 jit_solution(16203545664998103106)
XLA Ops:
  0.6 4.4 %shard_map.50 = (f32[16,4,128]{2,1,0:T(4,128)}, bf16[512,128]{1,0:T(8,128)(2,1)}) custom-call(bf16[2048,128]{1,0:T(8,128)(2,1)} %tok_ref.1, bf16[512,128]{1,0:T(8,128)(2,1)} %cent_ref.1, f32[1,128]{1,0:T(1,128)} %bitcast.3), custom_call_target="tpu_custom_call" | custom-call | tf_op jit(solution)/shard_map/pallas_call | solution.py:188
  5.1 11.8 %all-to-all-start = ((f32[16,4,128]{2,1,0:T(4,128)}), f32[16,4,128]{2,1,0:T(4,128)S(1)}, u32[]{:S(2)}, u32[]{:S(2)}) async-start(f32[16,4,128]{2,1,0:T(4,128)} %get-tuple-element.18), calls=%async_computation | async-start | bytes 65536 | tf_op jit(solution)/shard_map/all_to_all | solution.py:212
  16.9 0.0 copy-start
  16.9 1.0 copy-done
  17.9 0.0 copy-start.1
  17.9 0.9 copy-done.1
  18.8 0.0 copy-start.2
  18.8 0.9 copy-done.2
  19.8 0.0 copy-start.3
  19.8 0.7 copy-done.3
  20.4 0.8 shard_map.51
  21.2 3.1 %all-to-all-done.parts_ref = f32[16,4,128]{2,1,0:T(4,128)S(1)} async-done(((f32[16,4,128]{2,1,0:T(4,128)}), f32[16,4,128]{2,1,0:T(4,128)S(1)}, u32[]{:S(2)}, u32[]{:S(2)}) %all-to-all-start) | async-done | bytes 32800 | tf_op jit(solution)/shard_map/all_to_all | solution.py:212
  24.3 1.6 %shard_map.52 = (bf16[512,2048]{1,0:T(8,128)(2,1)S(1)}, f32[16,128]{1,0:T(8,128)S(1)}, f32[32,16,128]{2,1,0:T(8,128)S(1)}) custom-call(f32[16,4,128]{2,1,0:T(4,128)S(1)} %all-to-all-done.parts_ref, bf16[2048,128]{1,0:T(8,128)(2,1)S(1)} %get-tuple-element.20.tok_ref, bf16[512,128]{1,0:T(8,128)(2,1)S(1)} %get-tuple-element.21.half_ref, ...), custom_call_target="tpu_custom_call" | custom-call | tf_op jit(solution)/shard_map/pallas_call | solution.py:188
  25.9 19.1 %all_to_all.40.parts_ref = f32[32,16,128]{2,1,0:T(8,128)S(1)} all-to-all(f32[32,16,128]{2,1,0:T(8,128)S(1)} %get-tuple-element.24), channel_id=1, replica_groups=mesh['dp'=16,'cent'=32] {'cent'}, dimensions={0} | all-to-all | bytes 524288 | tf_op jit(solution)/shard_map/all_to_all | solution.py:212
  45.1 0.7 shard_map.53
  45.8 14.7 %all_to_all.41.parts_ref = f32[16,4,128]{2,1,0:T(4,128)S(1)} all-to-all(f32[16,4,128]{2,1,0:T(4,128)S(1)} %get-tuple-element.27), channel_id=1, replica_groups=mesh['dp'=16,'cent'=32] {'dp'}, dimensions={0} | all-to-all | bytes 65536 | tf_op jit(solution)/shard_map/all_to_all | solution.py:212
  60.5 0.6 shard_map.54
  61.1 13.6 %all_to_all.42.parts_ref = f32[32,16,128]{2,1,0:T(8,128)S(1)} all-to-all(f32[32,16,128]{2,1,0:T(8,128)S(1)} %get-tuple-element.29), channel_id=1, replica_groups=mesh['dp'=16,'cent'=32] {'cent'}, dimensions={0} | all-to-all | bytes 524288 | tf_op jit(solution)/shard_map/all_to_all | solution.py:212
  74.7 0.7 shard_map.55
  75.4 13.6 %all_to_all.43.parts_ref = f32[16,4,128]{2,1,0:T(4,128)S(1)} all-to-all(f32[16,4,128]{2,1,0:T(4,128)S(1)} %shard_map.55), channel_id=1, replica_groups=mesh['dp'=16,'cent'=32] {'dp'}, dimensions={0} | all-to-all | bytes 65536 | tf_op jit(solution)/shard_map/all_to_all | solution.py:212
  88.9 0.4 shard_map.56
  89.4 13.6 %all_to_all.44.parts_ref = f32[32,16,128]{2,1,0:T(8,128)S(1)} all-to-all(f32[32,16,128]{2,1,0:T(8,128)S(1)} %get-tuple-element.30), channel_id=1, replica_groups=mesh['dp'=16,'cent'=32] {'cent'}, dimensions={0} | all-to-all | bytes 524288 | tf_op jit(solution)/shard_map/all_to_all | solution.py:212
  103.0 0.9 shard_map.57
  103.8 19.2 %all_to_all.45.parts_ref = f32[16,40,128]{2,1,0:T(8,128)S(1)} all-to-all(f32[16,40,128]{2,1,0:T(8,128)S(1)} %shard_map.57), channel_id=1, replica_groups=mesh['dp'=16,'cent'=32] {'dp'}, dimensions={0} | all-to-all | bytes 655360 | tf_op jit(solution)/shard_map/all_to_all | solution.py:212
  123.0 0.6 shard_map.58
  123.6 14.5 %all_to_all.46 = f32[16,32,128]{2,1,0:T(8,128)S(1)} all-to-all(f32[16,32,128]{2,1,0:T(8,128)S(1)} %get-tuple-element.32), channel_id=1, replica_groups=mesh['dp'=16,'cent'=32] {'dp'}, dimensions={0} | all-to-all | bytes 524288 | tf_op jit(solution)/shard_map/all_to_all | solution.py:212
  138.1 0.7 copy.6
Async XLA Ops:
  5.1 19.2 %all-to-all-start = ((f32[16,4,128]{2,1,0:T(4,128)}), f32[16,4,128]{2,1,0:T(4,128)S(1)}, u32[]{:S(2)}, u32[]{:S(2)}) async-start(f32[16,4,128]{2,1,0:T(4,128)} %get-tuple-element.18), calls=%async_computation | async-start | bytes 65536 | tf_op jit(solution)/shard_map/all_to_all | solution.py:212
  16.9 1.0 copy-start
  17.9 0.9 copy-start.1
  18.8 0.9 copy-start.2
  19.8 0.7 copy-start.3

commit v4 on v3

--- a/solution.py
+++ b/solution.py
@@ -69,25 +69,25 @@
     out_ref[...] = jnp.broadcast_to(dense[None], out_ref.shape)
 
 
-def first_columns(tok_hbm, cent_hbm, diag_hbm, out_ref, half_ref, tok_ref, cent_ref, diag_ref, sems):
+def half_scaled(cent_ref, diag):
+    scaled = (cent_ref[...].astype(F32) * diag).astype(BF16)
+    return (0.5 * scaled.astype(F32)).astype(BF16)
+
+
+def first_columns(tok_hbm, cent_hbm, diag_hbm, out_ref, began_ref, tok_ref, cent_ref, diag_ref, sems):
     loads = [
         pltpu.make_async_copy(cent_hbm, cent_ref, sems.at[0]),
         pltpu.make_async_copy(diag_hbm, diag_ref, sems.at[1]),
+        pltpu.make_async_copy(tok_hbm, tok_ref, sems.at[2]),
     ]
-    tiles = []
-    for k in range(tok_ref.shape[0] // TILE):
-        at = pl.ds(k * TILE, TILE)
-        tiles.append(pltpu.make_async_copy(tok_hbm.at[at], tok_ref.at[at], sems.at[2 + k]))
-    for load in loads + tiles:
+    for load in loads:
         load.start()
     for load in loads:
         load.wait()
     diag = diag_ref[...]
-    half = (0.5 * (cent_ref[...].astype(F32) * diag).astype(BF16).astype(F32)).astype(BF16)
-    half_ref[...] = half
+    half = half_scaled(cent_ref, diag)
     top = total = None
-    for k, load in enumerate(tiles):
-        load.wait()
+    for k in range(tok_ref.shape[0] // TILE):
         tok = tok_ref[k * TILE : (k + 1) * TILE, :]
         wide = tok.astype(F32)
         norm = 0.25 * jnp.sum(wide * wide * diag, axis=1, keepdims=True)
@@ -98,6 +98,7 @@
         total = part if top is None else total * jnp.exp(top - new) + part
         top = new
     spread_out(out_ref, dense_rows(top + jnp.log(total)))
+    began_ref[...] = jnp.zeros_like(began_ref)
 
 
 def dense_norms(vectors_ref, diag, out_ref):
@@ -107,11 +108,13 @@
         out_ref[k : k + 1, :] = jnp.broadcast_to(norm, (LANES, LANES)).T[:1]
 
 
-def prepare(tok_ref, cent_ref, diag_ref, half_ref, near_ref, near_half_ref, tok_norm_ref, cent_norm_ref):
+def prepare(tok_ref, cent_ref, diag_ref, after_ref, near_ref, half_ref, tok_norm_ref, cent_norm_ref):
+    del after_ref
+    diag = diag_ref[...]
     near_ref[...] = tok_ref[...]
-    near_half_ref[...] = half_ref[...]
-    dense_norms(tok_ref, diag_ref[...], tok_norm_ref)
-    dense_norms(cent_ref, diag_ref[...], cent_norm_ref)
+    half_ref[...] = half_scaled(cent_ref, diag)
+    dense_norms(tok_ref, diag, tok_norm_ref)
+    dense_norms(cent_ref, diag, cent_norm_ref)
 
 
 def first_rows(
@@ -144,9 +147,10 @@
     spread_out(out_ref, column_sums(kept_ref, gain))
 
 
-def later_rows(ratio, parts_ref, gain_ref, kept_ref, out_ref, scale_ref):
+def later_rows(ratio, parts_ref, gain_ref, kept_ref, out_ref, *scale_ref):
     scale = ratio / jnp.sum(parts_ref[...], axis=0)
-    scale_ref[...] = scale
+    if scale_ref:
+        scale_ref[0][...] = scale
     spread_out(out_ref, gain_ref[...] * row_sums(kept_ref, scale))
 
 
@@ -184,12 +188,32 @@
     spread_out(out_ref, total[:rows] / own)
 
 
-def run(kernel, outs, *operands, scratch=(), place=pltpu.VMEM, room=24, cost=0):
+def finish(cent_ref, mass_ref, cent_hbm, mass_hbm, sems):
+    stores = [
+        pltpu.make_async_copy(cent_ref, cent_hbm, sems.at[0]),
+        pltpu.make_async_copy(mass_ref, mass_hbm, sems.at[1]),
+    ]
+    for store in stores:
+        store.start()
+    for store in stores:
+        store.wait()
+
+
+def run(
+    kernel,
+    outs,
+    *operands,
+    scratch=(),
+    place=pltpu.VMEM,
+    out_place=pltpu.VMEM,
+    room=24,
+    cost=0,
+):
     return pl.pallas_call(
         kernel,
         out_shape=[jax.ShapeDtypeStruct(shape, kind) for shape, kind in outs],
         in_specs=[pl.BlockSpec(memory_space=place)] * len(operands),
-        out_specs=[pl.BlockSpec(memory_space=pltpu.VMEM)] * len(outs),
+        out_specs=[pl.BlockSpec(memory_space=out_place)] * len(outs),
         scratch_shapes=list(scratch),
         cost_estimate=pl.CostEstimate(flops=cost, bytes_accessed=cost, transcendentals=0)
         if cost
@@ -212,9 +236,9 @@
         return lax.all_to_all(copies, axis, 0, 0)
 
     diag = diagonal_factors.reshape(1, dim)
-    copies, half = run(
+    copies, began = run(
         first_columns,
-        [(to_dp, F32), ((cent_local, dim), BF16)],
+        [(to_dp, F32), ((8, LANES), F32)],
         tokens,
         centroids,
         diag,
@@ -222,18 +246,18 @@
             pltpu.VMEM((tok_local, dim), BF16),
             pltpu.VMEM((cent_local, dim), BF16),
             pltpu.VMEM((1, dim), F32),
-            pltpu.SemaphoreType.DMA((2 + tok_local // TILE,)),
+            pltpu.SemaphoreType.DMA((3,)),
         ],
         place=pltpu.HBM,
         room=60,
     )
-    near, near_half, tok_norm, cent_norm = run(
+    near, half, tok_norm, cent_norm = run(
         prepare,
         [((tok_local, dim), BF16), ((cent_local, dim), BF16), (by_tok, F32), (by_cent, F32)],
         tokens,
         centroids,
         diag,
-        half,
+        began,
         cost=4 * (tok_local + cent_local) * dim,
     )
     kept, top, copies = run(
@@ -241,7 +265,7 @@
         [((cent_local, tok_local), BF16), (by_tok, F32), (to_cent, F32)],
         over("dp", copies),
         near,
-        near_half,
+        half,
         cent_norm,
         tok_norm,
         scratch=[pltpu.VMEM(by_tok, F32)],
@@ -255,7 +279,7 @@
     )
     rows_of = functools.partial(later_rows, ratio)
     rows_outs = [(to_cent, F32), (by_cent, F32)]
-    copies, scale = run(rows_of, rows_outs, over("dp", copies), gain, kept)
+    (copies,) = run(rows_of, rows_outs[:1], over("dp", copies), gain, kept)
     (copies,) = run(later_columns, [(to_dp, F32)], over("cent", copies), gain, kept)
     copies, scale = run(rows_of, rows_outs, over("dp", copies), gain, kept)
 
@@ -274,7 +298,14 @@
         over("dp", copies),
         scale,
     )
-    new_centroids = over("dp", copies).reshape(cent_local, dim)
+    new_centroids, masses = run(
+        finish,
+        [((cent_local, dim), F32), (by_cent, F32)],
+        over("dp", copies).reshape(cent_local, dim),
+        masses,
+        scratch=[pltpu.SemaphoreType.DMA((2,))],
+        out_place=pltpu.HBM,
+    )
     return (new_centroids, masses.reshape(cent_local))
 
 

time: 139 us -> 137 us (0.986)
    pallas_call x9 -> x10, Pallas kernels: 10.7 us -> 9.59 us  [run(): pl.pallas_call(kernel, out_shape=[jax.ShapeDtypeStruct(shape, kind) for s...]
    unnamed x9 -> x8, local copies, waits for them, and re-layouts: 4.2 us -> 3.27 us
where the time goes in v4:
time: 137 us
  blocking collectives  108 us (79%)
  starting transfers between devices  11.8 us (9%)
  Pallas kernels  9.59 us (7%)
  waiting for transfers between devices  3.31 us (2%)
  local copies, waits for them, and re-layouts  3.27 us (2%)
    all_to_all x7, blocking collectives, over(): return lax.all_to_all(copies, axis, 0, 0)  108 us
    all_to_all x1, starting transfers between devices, over(): return lax.all_to_all(copies, axis, 0, 0)  11.8 us
    pallas_call x10, Pallas kernels, run(): pl.pallas_call(kernel, out_shape=[jax.ShapeDtypeStruct(shape, kind) for s...  9.59 us
    all_to_all x1, waiting for transfers between devices, over(): return lax.all_to_all(copies, axis, 0, 0)  3.31 us
    unnamed x8, local copies, waits for them, and re-layouts  3.27 us
  transfers between devices with their start and end apart: 1, of which 1 were waited for; matrix products, arithmetic and copies ran while one was open for 0% of the time, Pallas kernels for 1%

profile of v4, /device:TPU:1, one launch (start us, length us, event | category | flops | bytes accessed | tf_op | source)
XLA Modules:
  0.0 136.8 jit_solution(3194479913507711894)
XLA Ops:
  0.6 3.3 %shard_map.50 = (f32[16,4,128]{2,1,0:T(4,128)}, f32[8,128]{1,0:T(8,128)}) custom-call(bf16[2048,128]{1,0:T(8,128)(2,1)} %tok_ref.1, bf16[512,128]{1,0:T(8,128)(2,1)} %cent_ref.1, f32[1,128]{1,0:T(1,128)} %bitcast.4), custom_call_target="tpu_custom_call" | custom-call | tf_op jit(solution)/shard_map/pallas_call | solution.py:212
  3.9 11.8 %all-to-all-start = ((f32[16,4,128]{2,1,0:T(4,128)}), f32[16,4,128]{2,1,0:T(4,128)S(1)}, u32[]{:S(2)}, u32[]{:S(2)}) async-start(f32[16,4,128]{2,1,0:T(4,128)} %get-tuple-element.19), calls=%async_computation | async-start | bytes 65536 | tf_op jit(solution)/shard_map/all_to_all | solution.py:236
  15.8 0.0 copy-start
  15.8 1.0 copy-done
  16.8 0.0 copy-start.1
  16.8 0.9 copy-done.1
  17.7 0.0 copy-start.2
  17.7 0.7 copy-done.2
  18.4 0.0 copy-start.3
  18.4 0.7 copy-done.3
  19.0 0.8 shard_map.51
  19.8 3.3 %all-to-all-done.parts_ref = f32[16,4,128]{2,1,0:T(4,128)S(1)} async-done(((f32[16,4,128]{2,1,0:T(4,128)}), f32[16,4,128]{2,1,0:T(4,128)S(1)}, u32[]{:S(2)}, u32[]{:S(2)}) %all-to-all-start) | async-done | bytes 32800 | tf_op jit(solution)/shard_map/all_to_all | solution.py:236
  23.2 1.6 %shard_map.52 = (bf16[512,2048]{1,0:T(8,128)(2,1)S(1)}, f32[16,128]{1,0:T(8,128)S(1)}, f32[32,16,128]{2,1,0:T(8,128)S(1)}) custom-call(f32[16,4,128]{2,1,0:T(4,128)S(1)} %all-to-all-done.parts_ref, bf16[2048,128]{1,0:T(8,128)(2,1)S(1)} %get-tuple-element.21.tok_ref, bf16[512,128]{1,0:T(8,128)(2,1)S(1)} %get-tuple-element.22.half_ref, ...), custom_call_target="tpu_custom_call" | custom-call | tf_op jit(solution)/shard_map/pallas_call | solution.py:212
  24.8 19.1 %all_to_all.40.parts_ref = f32[32,16,128]{2,1,0:T(8,128)S(1)} all-to-all(f32[32,16,128]{2,1,0:T(8,128)S(1)} %get-tuple-element.25), channel_id=1, replica_groups=mesh['dp'=16,'cent'=32] {'cent'}, dimensions={0} | all-to-all | bytes 524288 | tf_op jit(solution)/shard_map/all_to_all | solution.py:236
  44.0 0.7 shard_map.53
  44.6 14.4 %all_to_all.41.parts_ref = f32[16,4,128]{2,1,0:T(4,128)S(1)} all-to-all(f32[16,4,128]{2,1,0:T(4,128)S(1)} %get-tuple-element.28), channel_id=1, replica_groups=mesh['dp'=16,'cent'=32] {'dp'}, dimensions={0} | all-to-all | bytes 65536 | tf_op jit(solution)/shard_map/all_to_all | solution.py:236
  59.1 0.4 shard_map.54
  59.5 13.6 %all_to_all.42.parts_ref = f32[32,16,128]{2,1,0:T(8,128)S(1)} all-to-all(f32[32,16,128]{2,1,0:T(8,128)S(1)} %shard_map.54), channel_id=1, replica_groups=mesh['dp'=16,'cent'=32] {'cent'}, dimensions={0} | all-to-all | bytes 524288 | tf_op jit(solution)/shard_map/all_to_all | solution.py:236
  73.1 0.7 shard_map.55
  73.8 13.6 %all_to_all.43.parts_ref = f32[16,4,128]{2,1,0:T(4,128)S(1)} all-to-all(f32[16,4,128]{2,1,0:T(4,128)S(1)} %shard_map.55), channel_id=1, replica_groups=mesh['dp'=16,'cent'=32] {'dp'}, dimensions={0} | all-to-all | bytes 65536 | tf_op jit(solution)/shard_map/all_to_all | solution.py:236
  87.4 0.4 shard_map.56
  87.8 13.6 %all_to_all.44.parts_ref = f32[32,16,128]{2,1,0:T(8,128)S(1)} all-to-all(f32[32,16,128]{2,1,0:T(8,128)S(1)} %get-tuple-element.30), channel_id=1, replica_groups=mesh['dp'=16,'cent'=32] {'cent'}, dimensions={0} | all-to-all | bytes 524288 | tf_op jit(solution)/shard_map/all_to_all | solution.py:236
  101.4 0.9 shard_map.57
  102.3 19.2 %all_to_all.45.parts_ref = f32[16,40,128]{2,1,0:T(8,128)S(1)} all-to-all(f32[16,40,128]{2,1,0:T(8,128)S(1)} %shard_map.57), channel_id=1, replica_groups=mesh['dp'=16,'cent'=32] {'dp'}, dimensions={0} | all-to-all | bytes 655360 | tf_op jit(solution)/shard_map/all_to_all | solution.py:236
  121.5 0.1 shard_map.58
  121.6 14.5 %all_to_all.46 = f32[16,32,128]{2,1,0:T(8,128)S(1)} all-to-all(f32[16,32,128]{2,1,0:T(8,128)S(1)} %get-tuple-element.32), channel_id=1, replica_groups=mesh['dp'=16,'cent'=32] {'dp'}, dimensions={0} | all-to-all | bytes 524288 | tf_op jit(solution)/shard_map/all_to_all | solution.py:236
  136.1 0.7 shard_map.59
Async XLA Ops:
  3.9 19.2 %all-to-all-start = ((f32[16,4,128]{2,1,0:T(4,128)}), f32[16,4,128]{2,1,0:T(4,128)S(1)}, u32[]{:S(2)}, u32[]{:S(2)}) async-start(f32[16,4,128]{2,1,0:T(4,128)} %get-tuple-element.19), calls=%async_computation | async-start | bytes 65536 | tf_op jit(solution)/shard_map/all_to_all | solution.py:236
  15.8 1.0 copy-start
  16.8 0.9 copy-start.1
  17.7 0.7 copy-start.2
  18.4 0.7 copy-start.3

commit v5 on v4

--- a/solution.py
+++ b/solution.py
@@ -6,10 +6,12 @@
 from jax import lax
 from jax.experimental import pallas as pl
 from jax.experimental.pallas import tpu as pltpu
+from jax.sharding import Mesh
 from jax.sharding import PartitionSpec as P
 
 LANES = 128
 TILE = 256
+DP = ("z", "core")
 F32 = jnp.float32
 BF16 = jnp.bfloat16
 
@@ -189,10 +191,10 @@
 
 
 def finish(cent_ref, mass_ref, cent_hbm, mass_hbm, sems):
-    stores = [
-        pltpu.make_async_copy(cent_ref, cent_hbm, sems.at[0]),
-        pltpu.make_async_copy(mass_ref, mass_hbm, sems.at[1]),
-    ]
+    cores = cent_ref.shape[0]
+    stores = [pltpu.make_async_copy(mass_ref, mass_hbm, sems.at[cores])]
+    for c in range(cores):
+        stores.append(pltpu.make_async_copy(cent_ref.at[c], cent_hbm.at[:, c], sems.at[c]))
     for store in stores:
         store.start()
     for store in stores:
@@ -223,7 +225,8 @@
 
 
 def shards(tokens, centroids, diagonal_factors):
-    dp, cent = lax.axis_size("dp"), lax.axis_size("cent")
+    chips, cores, cent = (lax.axis_size(axis) for axis in ("z", "core", "cent"))
+    dp = chips * cores
     tok_local, dim = tokens.shape
     cent_local = centroids.shape[0]
     cent_count = cent_local * cent
@@ -263,7 +266,7 @@
     kept, top, copies = run(
         functools.partial(first_rows, cent_count),
         [((cent_local, tok_local), BF16), (by_tok, F32), (to_cent, F32)],
-        over("dp", copies),
+        over(DP, copies),
         near,
         half,
         cent_norm,
@@ -279,9 +282,9 @@
     )
     rows_of = functools.partial(later_rows, ratio)
     rows_outs = [(to_cent, F32), (by_cent, F32)]
-    (copies,) = run(rows_of, rows_outs[:1], over("dp", copies), gain, kept)
+    (copies,) = run(rows_of, rows_outs[:1], over(DP, copies), gain, kept)
     (copies,) = run(later_columns, [(to_dp, F32)], over("cent", copies), gain, kept)
-    copies, scale = run(rows_of, rows_outs, over("dp", copies), gain, kept)
+    copies, scale = run(rows_of, rows_outs, over(DP, copies), gain, kept)
 
     packed = (dp, rows + 8, LANES)
     (copies,) = run(
@@ -294,26 +297,29 @@
     )
     copies, masses = run(
         functools.partial(divide, rows, ratio),
-        [((dp, rows, dim), F32), (by_cent, F32)],
-        over("dp", copies),
+        [((chips, rows, dim), F32), (by_cent, F32)],
+        over(DP, copies),
         scale,
     )
+    halves = lax.all_gather(over("z", copies), "core")
     new_centroids, masses = run(
         finish,
-        [((cent_local, dim), F32), (by_cent, F32)],
-        over("dp", copies).reshape(cent_local, dim),
+        [((chips, cores, rows, dim), F32), (by_cent, F32)],
+        halves,
         masses,
-        scratch=[pltpu.SemaphoreType.DMA((2,))],
+        scratch=[pltpu.SemaphoreType.DMA((cores + 1,))],
         out_place=pltpu.HBM,
     )
-    return (new_centroids, masses.reshape(cent_local))
+    return (new_centroids.reshape(cent_local, dim), masses.reshape(cent_local))
 
 
 def solution(mesh):
+    dp, cent = mesh.devices.shape
+    split = Mesh(mesh.devices.reshape(dp // 2, 2, cent), DP + ("cent",))
     return jax.shard_map(
         shards,
-        mesh=mesh,
-        in_specs=(P("dp", None), P("cent", None), P()),
+        mesh=split,
+        in_specs=(P(DP, None), P("cent", None), P()),
         out_specs=(P("cent", None), P("cent")),
         check_vma=False,
     )

time: 137 us -> 137 us (level)
    all_to_all x7, blocking collectives: 108 us -> 104 us  [over(): return lax.all_to_all(copies, axis, 0, 0)]
    all_gather x0 -> x1, blocking collectives: none -> 3.26 us  [shards(): halves = lax.all_gather(over('z', copies), 'core')]
where the time goes in v5:
time: 137 us; the launch traced here: 136 us
  blocking collectives  108 us (79%)
  starting transfers between devices  11.8 us (9%)
  Pallas kernels  9.58 us (7%)
  waiting for transfers between devices  3.31 us (2%)
  local copies, waits for them, and re-layouts  3.27 us (2%)
    all_to_all x7, blocking collectives, over(): return lax.all_to_all(copies, axis, 0, 0)  104 us
    all_to_all x1, starting transfers between devices, over(): return lax.all_to_all(copies, axis, 0, 0)  11.8 us
    pallas_call x10, Pallas kernels, run(): pl.pallas_call(kernel, out_shape=[jax.ShapeDtypeStruct(shape, kind) for s...  9.58 us
    all_to_all x1, waiting for transfers between devices, over(): return lax.all_to_all(copies, axis, 0, 0)  3.31 us
    unnamed x8, local copies, waits for them, and re-layouts  3.27 us
    all_gather x1, blocking collectives, shards(): halves = lax.all_gather(over('z', copies), 'core')  3.26 us
  transfers between devices with their start and end apart: 1, of which 1 were waited for; matrix products, arithmetic and copies ran while one was open for 0% of the time, Pallas kernels for 1%

profile of v5, /device:TPU:1, one launch (start us, length us, event | category | flops | bytes accessed | tf_op | source)
XLA Modules:
  0.0 136.3 jit_solution(17073575676857225089)
XLA Ops:
  0.6 3.3 %shard_map.50 = (f32[16,4,128]{2,1,0:T(4,128)}, f32[8,128]{1,0:T(8,128)}) custom-call(bf16[2048,128]{1,0:T(8,128)(2,1)} %tok_ref.1, bf16[512,128]{1,0:T(8,128)(2,1)} %cent_ref.1, f32[1,128]{1,0:T(1,128)} %bitcast.5), custom_call_target="tpu_custom_call" | custom-call | tf_op jit(solution)/shard_map/pallas_call | solution.py:214
  3.9 11.8 %all-to-all-start = ((f32[16,4,128]{2,1,0:T(4,128)}), f32[16,4,128]{2,1,0:T(4,128)S(1)}, u32[]{:S(2)}, u32[]{:S(2)}) async-start(f32[16,4,128]{2,1,0:T(4,128)} %get-tuple-element.19), calls=%async_computation | async-start | bytes 65536 | tf_op jit(solution)/shard_map/all_to_all | solution.py:239
  15.8 0.0 copy-start
  15.8 1.0 copy-done
  16.8 0.0 copy-start.1
  16.8 0.9 copy-done.1
  17.7 0.0 copy-start.2
  17.7 0.7 copy-done.2
  18.4 0.0 copy-start.3
  18.4 0.7 copy-done.3
  19.0 0.8 shard_map.51
  19.8 3.3 %all-to-all-done.parts_ref = f32[16,4,128]{2,1,0:T(4,128)S(1)} async-done(((f32[16,4,128]{2,1,0:T(4,128)}), f32[16,4,128]{2,1,0:T(4,128)S(1)}, u32[]{:S(2)}, u32[]{:S(2)}) %all-to-all-start) | async-done | bytes 32800 | tf_op jit(solution)/shard_map/all_to_all | solution.py:239
  23.2 1.6 %shard_map.52 = (bf16[512,2048]{1,0:T(8,128)(2,1)S(1)}, f32[16,128]{1,0:T(8,128)S(1)}, f32[32,16,128]{2,1,0:T(8,128)S(1)}) custom-call(f32[16,4,128]{2,1,0:T(4,128)S(1)} %all-to-all-done.parts_ref, bf16[2048,128]{1,0:T(8,128)(2,1)S(1)} %get-tuple-element.21.tok_ref, bf16[512,128]{1,0:T(8,128)(2,1)S(1)} %get-tuple-element.22.half_ref, ...), custom_call_target="tpu_custom_call" | custom-call | tf_op jit(solution)/shard_map/pallas_call | solution.py:214
  24.8 19.1 %all_to_all.40.parts_ref = f32[32,16,128]{2,1,0:T(8,128)S(1)} all-to-all(f32[32,16,128]{2,1,0:T(8,128)S(1)} %get-tuple-element.25), channel_id=1, replica_groups=mesh['z'=8,'core'=2,'cent'=32] {'cent'}, dimensions={0} | all-to-all | bytes 524288 | tf_op jit(solution)/shard_map/all_to_all | solution.py:239
  43.9 0.7 shard_map.53
  44.6 14.4 %all_to_all.41.parts_ref = f32[16,4,128]{2,1,0:T(4,128)S(1)} all-to-all(f32[16,4,128]{2,1,0:T(4,128)S(1)} %get-tuple-element.28), channel_id=1, replica_groups=mesh['z'=8,'core'=2,'cent'=32] {'z','core'}, dimensions={0} | all-to-all | bytes 65536 | tf_op jit(solution)/shard_map/all_to_all | solution.py:239
  59.1 0.4 shard_map.54
  59.5 13.6 %all_to_all.42.parts_ref = f32[32,16,128]{2,1,0:T(8,128)S(1)} all-to-all(f32[32,16,128]{2,1,0:T(8,128)S(1)} %shard_map.54), channel_id=1, replica_groups=mesh['z'=8,'core'=2,'cent'=32] {'cent'}, dimensions={0} | all-to-all | bytes 524288 | tf_op jit(solution)/shard_map/all_to_all | solution.py:239
  73.1 0.7 shard_map.55
  73.8 13.6 %all_to_all.43.parts_ref = f32[16,4,128]{2,1,0:T(4,128)S(1)} all-to-all(f32[16,4,128]{2,1,0:T(4,128)S(1)} %shard_map.55), channel_id=1, replica_groups=mesh['z'=8,'core'=2,'cent'=32] {'z','core'}, dimensions={0} | all-to-all | bytes 65536 | tf_op jit(solution)/shard_map/all_to_all | solution.py:239
  87.4 0.4 shard_map.56
  87.8 13.6 %all_to_all.44.parts_ref = f32[32,16,128]{2,1,0:T(8,128)S(1)} all-to-all(f32[32,16,128]{2,1,0:T(8,128)S(1)} %get-tuple-element.30), channel_id=1, replica_groups=mesh['z'=8,'core'=2,'cent'=32] {'cent'}, dimensions={0} | all-to-all | bytes 524288 | tf_op jit(solution)/shard_map/all_to_all | solution.py:239
  101.4 0.9 shard_map.57
  102.3 19.2 %all_to_all.45.parts_ref = f32[16,40,128]{2,1,0:T(8,128)S(1)} all-to-all(f32[16,40,128]{2,1,0:T(8,128)S(1)} %shard_map.57), channel_id=1, replica_groups=mesh['z'=8,'core'=2,'cent'=32] {'z','core'}, dimensions={0} | all-to-all | bytes 655360 | tf_op jit(solution)/shard_map/all_to_all | solution.py:239
  121.5 0.1 shard_map.58
  121.6 10.8 %all_to_all.46 = f32[8,32,128]{2,1,0:T(8,128)S(1)} all-to-all(f32[8,32,128]{2,1,0:T(8,128)S(1)} %get-tuple-element.32), channel_id=1, replica_groups=mesh['z'=8,'core'=2,'cent'=32] {'z'}, dimensions={0} | all-to-all | bytes 262144 | tf_op jit(solution)/shard_map/all_to_all | solution.py:239
  132.3 3.3 %all-gather = f32[16,32,128]{2,1,0:T(8,128)S(1)} all-gather(f32[8,32,128]{2,1,0:T(8,128)S(1)} %all_to_all.46), channel_id=2, replica_groups=mesh['z'=8,'core'=2,'cent'=32] {'core'}, dimensions={0}, use_global_device_ids=true | all-gather | bytes 393216 | tf_op jit(solution)/shard_map/all_gather | solution.py:304
  135.6 0.7 shard_map.59
Async XLA Ops:
  3.9 19.2 %all-to-all-start = ((f32[16,4,128]{2,1,0:T(4,128)}), f32[16,4,128]{2,1,0:T(4,128)S(1)}, u32[]{:S(2)}, u32[]{:S(2)}) async-start(f32[16,4,128]{2,1,0:T(4,128)} %get-tuple-element.19), calls=%async_computation | async-start | bytes 65536 | tf_op jit(solution)/shard_map/all_to_all | solution.py:239
  15.8 1.0 copy-start
  16.8 0.9 copy-start.1
  17.7 0.7 copy-start.2
  18.4 0.7 copy-start.3

commit v6 on v5

--- a/solution.py
+++ b/solution.py
@@ -12,6 +12,7 @@
 LANES = 128
 TILE = 256
 DP = ("z", "core")
+CENT = ("outer", "inner", "y")
 F32 = jnp.float32
 BF16 = jnp.bfloat16
 
@@ -119,50 +120,106 @@
     dense_norms(cent_ref, diag, cent_norm_ref)
 
 
+def keep_rows(half, col, tok_ref, start, kept_ref, top_ref, sum_ref):
+    column = jnp.concatenate(
+        [jnp.broadcast_to(col[k : k + 1], (LANES, LANES)).T for k in range(col.shape[0])], axis=0
+    )
+    column = jnp.concatenate([column] * (TILE // LANES), axis=1)
+    for k in range(kept_ref.shape[1] // TILE):
+        tok = tok_ref[pl.ds(pl.multiple_of(start + k * TILE, TILE), TILE), :]
+        score = along_lanes(half, tok) + column
+        top = jnp.max(score, axis=0, keepdims=True)
+        kept = jnp.exp(score - top)
+        kept_ref[:, k * TILE : (k + 1) * TILE] = kept.astype(BF16)
+        total = None
+        if sum_ref is not None:
+            total = top + jnp.log(jnp.sum(kept, axis=0, keepdims=True))
+        for h in range(TILE // LANES):
+            at = k * (TILE // LANES) + h
+            top_ref[at : at + 1, :] = top[:, h * LANES : (h + 1) * LANES]
+            if sum_ref is not None:
+                sum_ref[at : at + 1, :] = total[:, h * LANES : (h + 1) * LANES]
+
+
 def first_rows(
-    cent_count, parts_ref, tok_ref, half_ref, norm_ref, tok_norm_ref, kept_ref, top_ref, out_ref, sum_ref
+    cent_count,
+    parts_ref,
+    tok_ref,
+    half_ref,
+    norm_ref,
+    tok_norm_ref,
+    kept_ref,
+    out_ref,
+    give_ref,
+    top_ref,
+    sum_ref,
 ):
     norm = norm_ref[...]
     col = (-math.log(cent_count) - (combine_lse(parts_ref) - norm)) - norm
-    column = jnp.concatenate(
-        [jnp.broadcast_to(col[k : k + 1], (LANES, LANES)).T for k in range(col.shape[0])], axis=0
-    )
-    column = jnp.concatenate([column] * (TILE // LANES), axis=1)
     half = half_ref[...]
-    for k in range(tok_ref.shape[0] // TILE):
-        score = along_lanes(half, tok_ref[k * TILE : (k + 1) * TILE, :]) + column
-        top = jnp.max(score, axis=0, keepdims=True)
-        kept = jnp.exp(score - top)
-        kept_ref[:, k * TILE : (k + 1) * TILE] = kept.astype(BF16)
-        total = top + jnp.log(jnp.sum(kept, axis=0, keepdims=True))
-        for h in range(TILE // LANES):
-            at = k * (TILE // LANES) + h
-            top_ref[at : at + 1, :] = top[:, h * LANES : (h + 1) * LANES]
-            sum_ref[at : at + 1, :] = total[:, h * LANES : (h + 1) * LANES]
-    top_ref[...] = top_ref[...] - tok_norm_ref[...]
+    give_ref[: half.shape[0], :] = half.astype(F32)
+    give_ref[half.shape[0] : half.shape[0] + 8, :] = jnp.concatenate([col, col], axis=0)[:8]
+    keep_rows(half, col, tok_ref, 0, kept_ref, top_ref, sum_ref)
+    give_ref[half.shape[0] + 8 :, :] = top_ref[...] - tok_norm_ref[...]
     spread_out(out_ref, sum_ref[...] - tok_norm_ref[...])
 
 
-def second_columns(parts_ref, top_ref, kept_ref, out_ref, gain_ref):
-    gain = jnp.exp(top_ref[...] - combine_lse(parts_ref))
+def neighbour_rows(give_ref, other_ref, half_ref, tok_ref, tok_norm_ref, kept_ref, tops_ref):
+    place = lax.axis_index("inner")
+    count = half_ref.shape[0]
+    groups = count // LANES
+    half = jnp.concatenate([half_ref[...], other_ref[:count, :].astype(BF16)], axis=0)
+    col = jnp.concatenate(
+        [give_ref[count : count + groups, :], other_ref[count : count + groups, :]], axis=0
+    )
+    own, share = tok_norm_ref.shape[0], tok_norm_ref.shape[0] // 2
+    tops_ref[:own, :] = give_ref[give_ref.shape[0] - own :, :]
+    top_ref = tops_ref.at[own:]
+    keep_rows(half, col, tok_ref, place * kept_ref.shape[1], kept_ref, top_ref, None)
+    norm = tok_norm_ref[pl.ds(pl.multiple_of(place * share, share), share), :]
+    top_ref[...] = top_ref[...] - norm
+
+
+def choose(place, first, second):
+    return jnp.where(jnp.broadcast_to(place, first.shape) == 0, first, second)
+
+
+def second_columns(parts_ref, tops_ref, kept_ref, out_ref, gain_ref, near_gain_ref):
+    total = combine_lse(parts_ref)
+    own, share = gain_ref.shape[0], near_gain_ref.shape[0]
+    gain = jnp.exp(tops_ref[:own, :] - total)
     gain_ref[...] = gain
+    mine = choose(lax.axis_index("inner"), total[:share], total[share:])
+    near_gain_ref[...] = jnp.exp(tops_ref[own:, :] - mine)
     spread_out(out_ref, column_sums(kept_ref, gain))
 
 
 def later_rows(ratio, parts_ref, gain_ref, kept_ref, out_ref, *scale_ref):
-    scale = ratio / jnp.sum(parts_ref[...], axis=0)
+    place = lax.axis_index("inner")
+    parts = parts_ref[...]
+    both = jnp.sum(parts.reshape((parts.shape[0] // 2, 2) + parts.shape[1:]), axis=0)
+    scale = ratio / choose(place, both[0], both[1])
+    other = ratio / choose(place, both[1], both[0])
     if scale_ref:
         scale_ref[0][...] = scale
-    spread_out(out_ref, gain_ref[...] * row_sums(kept_ref, scale))
-
-
-def later_columns(parts_ref, gain_ref, kept_ref, out_ref):
-    weight = gain_ref[...] / jnp.sum(parts_ref[...], axis=0)
+    scales = jnp.concatenate([scale, other], axis=0)
+    spread_out(out_ref, gain_ref[...] * row_sums(kept_ref, scales))
+
+
+def all_rows(outer, parts_ref):
+    parts = parts_ref[...]
+    parts = parts.reshape((outer, 2, parts.shape[0] // (2 * outer)) + parts.shape[1:])
+    both = jnp.sum(jnp.sum(parts, axis=2), axis=0)
+    return jnp.concatenate([both[0], both[1]], axis=0)
+
+
+def later_columns(outer, parts_ref, gain_ref, kept_ref, out_ref):
+    weight = gain_ref[...] / all_rows(outer, parts_ref)
     spread_out(out_ref, column_sums(kept_ref, weight))
 
 
-def numerators(rows, parts_ref, gain_ref, kept_ref, tok_ref, out_ref):
-    weight = gain_ref[...] / jnp.sum(parts_ref[...], axis=0)
+def numerators(rows, outer, parts_ref, gain_ref, kept_ref, tok_ref, out_ref):
+    weight = gain_ref[...] / all_rows(outer, parts_ref)
     ones = jnp.ones((TILE, LANES), BF16)
     total = None
     for k in range(kept_ref.shape[1] // TILE):
@@ -225,8 +282,8 @@
 
 
 def shards(tokens, centroids, diagonal_factors):
-    chips, cores, cent = (lax.axis_size(axis) for axis in ("z", "core", "cent"))
-    dp = chips * cores
+    chips, cores, outer = (lax.axis_size(axis) for axis in ("z", "core", "outer"))
+    dp, cent = chips * cores, lax.axis_size(CENT)
     tok_local, dim = tokens.shape
     cent_local = centroids.shape[0]
     cent_count = cent_local * cent
@@ -234,6 +291,8 @@
     rows = cent_local // dp
     by_tok, by_cent = (tok_local // LANES, LANES), (cent_local // LANES, LANES)
     to_dp, to_cent = (dp,) + by_cent, (cent,) + by_tok
+    by_half = (by_tok[0] // 2, LANES)
+    to_both, to_half = (2 * dp,) + by_cent, (cent,) + by_half
 
     def over(axis, copies):
         return lax.all_to_all(copies, axis, 0, 0)
@@ -263,34 +322,56 @@
         began,
         cost=4 * (tok_local + cent_local) * dim,
     )
-    kept, top, copies = run(
+    kept, copies, give = run(
         functools.partial(first_rows, cent_count),
-        [((cent_local, tok_local), BF16), (by_tok, F32), (to_cent, F32)],
+        [
+            ((cent_local, tok_local), BF16),
+            (to_cent, F32),
+            ((cent_local + 8 + by_tok[0], dim), F32),
+        ],
         over(DP, copies),
         near,
         half,
         cent_norm,
         tok_norm,
-        scratch=[pltpu.VMEM(by_tok, F32)],
-    )
-    copies, gain = run(
+        scratch=[pltpu.VMEM(by_tok, F32)] * 2,
+    )
+    other = lax.ppermute(give, "inner", [(0, 1), (1, 0)])
+    near_kept, tops = run(
+        neighbour_rows,
+        [((2 * cent_local, tok_local // 2), BF16), ((by_tok[0] + by_half[0], LANES), F32)],
+        give,
+        other,
+        half,
+        near,
+        tok_norm,
+        cost=cent_local * tok_local * 2 * dim,
+    )
+    copies, gain, near_gain = run(
         second_columns,
-        [(to_dp, F32), (by_tok, F32)],
-        over("cent", copies),
-        top,
+        [(to_both, F32), (by_tok, F32), (by_half, F32)],
+        over(CENT, copies),
+        tops,
         kept,
     )
     rows_of = functools.partial(later_rows, ratio)
-    rows_outs = [(to_cent, F32), (by_cent, F32)]
-    (copies,) = run(rows_of, rows_outs[:1], over(DP, copies), gain, kept)
-    (copies,) = run(later_columns, [(to_dp, F32)], over("cent", copies), gain, kept)
-    copies, scale = run(rows_of, rows_outs, over(DP, copies), gain, kept)
+    rows_outs = [(to_half, F32), (by_cent, F32)]
+    both = DP + ("inner",)
+    (copies,) = run(
+        rows_of, rows_outs[:1], over(both, copies), near_gain, near_kept
+    )
+    (copies,) = run(
+        functools.partial(later_columns, outer), [(to_both, F32)], over(CENT, copies), gain, kept
+    )
+    copies, scale = run(
+        rows_of, rows_outs, over(both, copies), near_gain, near_kept
+    )
 
     packed = (dp, rows + 8, LANES)
     (copies,) = run(
-        functools.partial(numerators, rows),
+        functools.partial(numerators, rows, outer),
         [(packed, F32)],
-        over("cent", copies),
+        over(CENT, copies),
         gain,
         kept,
         near,
@@ -315,11 +396,13 @@
 
 def solution(mesh):
     dp, cent = mesh.devices.shape
-    split = Mesh(mesh.devices.reshape(dp // 2, 2, cent), DP + ("cent",))
+    along_y = max(1, cent // 4)
+    shape = (dp // 2, 2, cent // (2 * along_y), 2, along_y)
+    split = Mesh(mesh.devices.reshape(shape), DP + CENT)
     return jax.shard_map(
         shards,
         mesh=split,
-        in_specs=(P(DP, None), P("cent", None), P()),
-        out_specs=(P("cent", None), P("cent")),
+        in_specs=(P(DP, None), P(CENT, None), P()),
+        out_specs=(P(CENT, None), P(CENT)),
         check_vma=False,
     )

time: 137 us -> 142 us (1.036)
  blocking collectives: 108 us -> 87.9 us
  starting transfers between devices: 11.8 us -> 24.7 us
  waiting for transfers between devices: 3.31 us -> 12.2 us
  Pallas kernels: 9.58 us -> 11.6 us
    all_to_all x7 -> x6, blocking collectives: 104 us -> 84.7 us  [over(): return lax.all_to_all(copies, axis, 0, 0)]
    all_to_all x1 -> x2, starting transfers between devices: 11.8 us -> 21.5 us  [over(): return lax.all_to_all(copies, axis, 0, 0)]
    ppermute x0 -> x1, waiting for transfers between devices: none -> 8.92 us  [shards(): other = lax.ppermute(give, 'inner', [(0, 1), (1, 0)])]
    ppermute x0 -> x1, starting transfers between devices: none -> 3.14 us  [shards(): other = lax.ppermute(give, 'inner', [(0, 1), (1, 0)])]
    pallas_call x10 -> x11, Pallas kernels: 9.58 us -> 11.6 us  [run(): pl.pallas_call(kernel, out_shape=[jax.ShapeDtypeStruct(shape, kind) for s...]
    unnamed x8 -> x12, local copies, waits for them, and re-layouts: 3.27 us -> 4.61 us
    all_to_all x1 -> x2, waiting for transfers between devices: 3.31 us -> 3.3 us  [over(): return lax.all_to_all(copies, axis, 0, 0)]
  transfers between devices with their start and end apart: 1 -> 3, of which waited for: 1 -> 2; matrix products, arithmetic and copies ran while one was open for 0% -> 0% of each run, Pallas kernels for 1% -> 2%
where the time goes in v6:
time: 142 us
  blocking collectives  87.9 us (62%)
  starting transfers between devices  24.7 us (17%)
  waiting for transfers between devices  12.2 us (9%)
  Pallas kernels  11.6 us (8%)
  local copies, waits for them, and re-layouts  4.61 us (3%)
    all_to_all x6, blocking collectives, over(): return lax.all_to_all(copies, axis, 0, 0)  84.7 us
    all_to_all x2, starting transfers between devices, over(): return lax.all_to_all(copies, axis, 0, 0)  21.5 us
    pallas_call x11, Pallas kernels, run(): pl.pallas_call(kernel, out_shape=[jax.ShapeDtypeStruct(shape, kind) for s...  11.6 us
    ppermute x1, waiting for transfers between devices, shards(): other = lax.ppermute(give, 'inner', [(0, 1), (1, 0)])  8.92 us
    unnamed x12, local copies, waits for them, and re-layouts  4.61 us
    all_to_all x2, waiting for transfers between devices, over(): return lax.all_to_all(copies, axis, 0, 0)  3.3 us
    all_gather x1, blocking collectives, shards(): halves = lax.all_gather(over('z', copies), 'core')  3.26 us
    ppermute x1, starting transfers between devices, shards(): other = lax.ppermute(give, 'inner', [(0, 1), (1, 0)])  3.14 us
  transfers between devices with their start and end apart: 3, of which 2 were waited for; matrix products, arithmetic and copies ran while one was open for 0% of the time, Pallas kernels for 2%

profile of v6, /device:TPU:1, one launch (start us, length us, event | category | flops | bytes accessed | tf_op | source)
XLA Modules:
  0.0 141.7 jit_solution(13756372819255705909)
XLA Ops:
  0.6 3.3 %shard_map.50 = (f32[16,4,128]{2,1,0:T(4,128)}, f32[8,128]{1,0:T(8,128)}) custom-call(bf16[2048,128]{1,0:T(8,128)(2,1)} %tok_ref.1, bf16[512,128]{1,0:T(8,128)(2,1)} %cent_ref.1, f32[1,128]{1,0:T(1,128)} %bitcast.5), custom_call_target="tpu_custom_call" | custom-call | tf_op jit(solution)/shard_map/pallas_call | solution.py:271
  3.9 11.8 %all-to-all-start = ((f32[16,4,128]{2,1,0:T(4,128)}), f32[16,4,128]{2,1,0:T(4,128)S(1)}, u32[]{:S(2)}, u32[]{:S(2)}) async-start(f32[16,4,128]{2,1,0:T(4,128)} %get-tuple-element.22), calls=%async_computation | async-start | bytes 65536 | tf_op jit(solution)/shard_map/all_to_all | solution.py:298
  15.8 0.0 copy-start.2
  15.8 1.0 copy-done.2
  16.8 0.0 copy-start.3
  16.8 0.9 copy-done.3
  17.7 0.0 copy-start.4
  17.7 0.7 copy-done.4
  18.4 0.0 copy-start.5
  18.4 0.7 copy-done.5
  19.0 0.8 shard_map.51
  19.9 3.3 %all-to-all-done.parts_ref = f32[16,4,128]{2,1,0:T(4,128)S(1)} async-done(((f32[16,4,128]{2,1,0:T(4,128)}), f32[16,4,128]{2,1,0:T(4,128)S(1)}, u32[]{:S(2)}, u32[]{:S(2)}) %all-to-all-start) | async-done | bytes 32800 | tf_op jit(solution)/shard_map/all_to_all | solution.py:298
  23.2 2.3 %shard_map.52 = (bf16[512,2048]{1,0:T(8,128)(2,1)S(1)}, f32[32,16,128]{2,1,0:T(8,128)}, f32[536,128]{1,0:T(8,128)S(1)}) custom-call(f32[16,4,128]{2,1,0:T(4,128)S(1)} %all-to-all-done.parts_ref, bf16[2048,128]{1,0:T(8,128)(2,1)S(1)} %get-tuple-element.24.tok_ref, bf16[512,128]{1,0:T(8,128)(2,1)S(1)} %get-tuple-element.25.half_ref, ...), custom_call_target="tpu_custom_call" | custom-call | tf_op jit(solution)/shard_map/pallas_call | solution.py:271
  25.5 9.7 %all-to-all-start.1 = ((f32[32,16,128]{2,1,0:T(8,128)}), f32[32,16,128]{2,1,0:T(8,128)S(1)}, u32[]{:S(2)}, u32[]{:S(2)}) async-start(f32[32,16,128]{2,1,0:T(8,128)} %get-tuple-element.28), calls=%async_computation.1 | async-start | bytes 524288 | tf_op jit(solution)/shard_map/all_to_all | solution.py:298
  35.1 3.1 %collective-permute-start = (f32[536,128]{1,0:T(8,128)S(1)}, f32[536,128]{1,0:T(8,128)S(1)}, u32[]{:S(2)}, u32[]{:S(2)}) collective-permute-start(f32[536,128]{1,0:T(8,128)S(1)} %get-tuple-element.29.give_ref), channel_id=1, source_target_pairs={{0,8},{8,0},{1,9},{9,1},{2,10},{10,2},{3,11},{11,3},{4,12},{12,4},... | collective-permute-start | bytes 823304 | tf_op jit(solution)/shard_map/ppermute | solution.py:339
  38.3 8.9 %collective-permute-done.other_ref = f32[536,128]{1,0:T(8,128)S(1)} collective-permute-done((f32[536,128]{1,0:T(8,128)S(1)}, f32[536,128]{1,0:T(8,128)S(1)}, u32[]{:S(2)}, u32[]{:S(2)}) %collective-permute-start) | collective-permute-done | bytes 274464 | tf_op jit(solution)/shard_map/ppermute | solution.py:339
  47.2 1.3 shard_map.53
  48.6 0.0 copy-start
  48.6 1.3 copy-done
  49.9 0.0 all-to-all-done.1.parts_ref
  49.9 0.0 copy-start.1
  49.9 0.7 shard_map.54
  50.6 13.3 %all_to_all.40.parts_ref = f32[32,4,128]{2,1,0:T(4,128)S(1)} all-to-all(f32[32,4,128]{2,1,0:T(4,128)S(1)} %get-tuple-element.32), channel_id=1, replica_groups=mesh['z'=8,'core'=2,'outer'=2,'inner'=2,'y'=8] {'z','core','inner'}, dimensions={0} | all-to-all | bytes 131072 | tf_op jit(solution)/shard_map/all_to_all | solution.py:298
  63.9 0.0 copy-done.1
  63.9 0.4 shard_map.55
  64.4 17.0 %all_to_all.41.parts_ref = f32[32,8,128]{2,1,0:T(8,128)S(1)} all-to-all(f32[32,8,128]{2,1,0:T(8,128)S(1)} %shard_map.55), channel_id=1, replica_groups=mesh['z'=8,'core'=2,'outer'=2,'inner'=2,'y'=8] {'outer','inner','y'}, dimensions={0} | all-to-all | bytes 262144 | tf_op jit(solution)/shard_map/all_to_all | solution.py:298
  81.4 0.7 shard_map.56
  82.1 13.1 %all_to_all.42.parts_ref = f32[32,4,128]{2,1,0:T(4,128)S(1)} all-to-all(f32[32,4,128]{2,1,0:T(4,128)S(1)} %shard_map.56), channel_id=1, replica_groups=mesh['z'=8,'core'=2,'outer'=2,'inner'=2,'y'=8] {'z','core','inner'}, dimensions={0} | all-to-all | bytes 131072 | tf_op jit(solution)/shard_map/all_to_all | solution.py:298
  95.1 0.4 shard_map.57
  95.6 12.8 %all_to_all.43.parts_ref = f32[32,8,128]{2,1,0:T(8,128)S(1)} all-to-all(f32[32,8,128]{2,1,0:T(8,128)S(1)} %get-tuple-element.36), channel_id=1, replica_groups=mesh['z'=8,'core'=2,'outer'=2,'inner'=2,'y'=8] {'outer','inner','y'}, dimensions={0} | all-to-all | bytes 262144 | tf_op jit(solution)/shard_map/all_to_all | solution.py:298
  108.4 0.8 shard_map.58
  109.2 17.7 %all_to_all.44.parts_ref = f32[16,40,128]{2,1,0:T(8,128)S(1)} all-to-all(f32[16,40,128]{2,1,0:T(8,128)S(1)} %shard_map.58), channel_id=1, replica_groups=mesh['z'=8,'core'=2,'outer'=2,'inner'=2,'y'=8] {'z','core'}, dimensions={0} | all-to-all | bytes 655360 | tf_op jit(solution)/shard_map/all_to_all | solution.py:298
  126.9 0.1 shard_map.59
  127.0 10.8 %all_to_all.45 = f32[8,32,128]{2,1,0:T(8,128)S(1)} all-to-all(f32[8,32,128]{2,1,0:T(8,128)S(1)} %get-tuple-element.38), channel_id=1, replica_groups=mesh['z'=8,'core'=2,'outer'=2,'inner'=2,'y'=8] {'z'}, dimensions={0} | all-to-all | bytes 262144 | tf_op jit(solution)/shard_map/all_to_all | solution.py:298
  137.7 3.3 %all-gather = f32[16,32,128]{2,1,0:T(8,128)S(1)} all-gather(f32[8,32,128]{2,1,0:T(8,128)S(1)} %all_to_all.45), channel_id=2, replica_groups=mesh['z'=8,'core'=2,'outer'=2,'inner'=2,'y'=8] {'core'}, dimensions={0}, use_global_device_ids=true | all-gather | bytes 393216 | tf_op jit(solution)/shard_map/all_gather | solution.py:385
  141.0 0.7 shard_map.60
Async XLA Ops:
  3.9 19.2 %all-to-all-start = ((f32[16,4,128]{2,1,0:T(4,128)}), f32[16,4,128]{2,1,0:T(4,128)S(1)}, u32[]{:S(2)}, u32[]{:S(2)}) async-start(f32[16,4,128]{2,1,0:T(4,128)} %get-tuple-element.22), calls=%async_computation | async-start | bytes 65536 | tf_op jit(solution)/shard_map/all_to_all | solution.py:298
  15.8 1.0 copy-start.2
  16.8 0.9 copy-start.3
  17.7 0.7 copy-start.4
  18.4 0.7 copy-start.5
  25.5 24.4 %all-to-all-start.1 = ((f32[32,16,128]{2,1,0:T(8,128)}), f32[32,16,128]{2,1,0:T(8,128)S(1)}, u32[]{:S(2)}, u32[]{:S(2)}) async-start(f32[32,16,128]{2,1,0:T(8,128)} %get-tuple-element.28), calls=%async_computation.1 | async-start | bytes 524288 | tf_op jit(solution)/shard_map/all_to_all | solution.py:298
  35.1 12.1 %collective-permute-start = (f32[536,128]{1,0:T(8,128)S(1)}, f32[536,128]{1,0:T(8,128)S(1)}, u32[]{:S(2)}, u32[]{:S(2)}) collective-permute-start(f32[536,128]{1,0:T(8,128)S(1)} %get-tuple-element.29.give_ref), channel_id=1, source_target_pairs={{0,8},{8,0},{1,9},{9,1},{2,10},{10,2},{3,11},{11,3},{4,12},{12,4},... | collective-permute-start | bytes 823304 | tf_op jit(solution)/shard_map/ppermute | solution.py:339
  48.6 1.3 copy-start
  49.9 14.0 %copy-start.1 = (bf16[1024,1024]{1,0:T(8,128)(2,1)S(1)}, bf16[1024,1024]{1,0:T(8,128)(2,1)}, u32[]{:S(2)}) copy-start(bf16[1024,1024]{1,0:T(8,128)(2,1)} %copy-done) | copy-start | bytes 6291460

commit v7 on v5

--- a/solution.py
+++ b/solution.py
@@ -11,7 +11,7 @@
 
 LANES = 128
 TILE = 256
-DP = ("z", "core")
+DP = ("core", "z")
 F32 = jnp.float32
 BF16 = jnp.bfloat16
 
@@ -194,7 +194,7 @@
     cores = cent_ref.shape[0]
     stores = [pltpu.make_async_copy(mass_ref, mass_hbm, sems.at[cores])]
     for c in range(cores):
-        stores.append(pltpu.make_async_copy(cent_ref.at[c], cent_hbm.at[:, c], sems.at[c]))
+        stores.append(pltpu.make_async_copy(cent_ref.at[c], cent_hbm.at[c], sems.at[c]))
     for store in stores:
         store.start()
     for store in stores:
@@ -304,7 +304,7 @@
     halves = lax.all_gather(over("z", copies), "core")
     new_centroids, masses = run(
         finish,
-        [((chips, cores, rows, dim), F32), (by_cent, F32)],
+        [((cores, chips, rows, dim), F32), (by_cent, F32)],
         halves,
         masses,
         scratch=[pltpu.SemaphoreType.DMA((cores + 1,))],
@@ -315,11 +315,11 @@
 
 def solution(mesh):
     dp, cent = mesh.devices.shape
-    split = Mesh(mesh.devices.reshape(dp // 2, 2, cent), DP + ("cent",))
+    split = Mesh(mesh.devices.reshape(dp // 2, 2, cent), ("z", "core", "cent"))
     return jax.shard_map(
         shards,
         mesh=split,
-        in_specs=(P(DP, None), P("cent", None), P()),
+        in_specs=(P(("z", "core"), None), P("cent", None), P()),
         out_specs=(P("cent", None), P("cent")),
         check_vma=False,
     )

time: 137 us -> 136 us (level)
    all_to_all x7, blocking collectives: 104 us -> 103 us  [over(): return lax.all_to_all(copies, axis, 0, 0)]
where the time goes in v7:
time: 136 us; the launch traced here: 135 us
  blocking collectives  107 us (79%)
  starting transfers between devices  11.8 us (9%)
  Pallas kernels  9.58 us (7%)
  local copies, waits for them, and re-layouts  3.27 us (2%)
  waiting for transfers between devices  2.96 us (2%)
    all_to_all x7, blocking collectives, over(): return lax.all_to_all(copies, axis, 0, 0)  103 us
    all_to_all x1, starting transfers between devices, over(): return lax.all_to_all(copies, axis, 0, 0)  11.8 us
    pallas_call x10, Pallas kernels, run(): pl.pallas_call(kernel, out_shape=[jax.ShapeDtypeStruct(shape, kind) for s...  9.58 us
    all_gather x1, blocking collectives, shards(): halves = lax.all_gather(over('z', copies), 'core')  3.89 us
    unnamed x8, local copies, waits for them, and re-layouts  3.27 us
    all_to_all x1, waiting for transfers between devices, over(): return lax.all_to_all(copies, axis, 0, 0)  2.96 us
  transfers between devices with their start and end apart: 1, of which 1 were waited for; matrix products, arithmetic and copies ran while one was open for 0% of the time, Pallas kernels for 1%

profile of v7, /device:TPU:1, one launch (start us, length us, event | category | flops | bytes accessed | tf_op | source)
XLA Modules:
  0.0 135.2 jit_solution(12363329987197187999)
XLA Ops:
  0.6 3.3 %shard_map.50 = (f32[16,4,128]{2,1,0:T(4,128)}, f32[8,128]{1,0:T(8,128)}) custom-call(bf16[2048,128]{1,0:T(8,128)(2,1)} %tok_ref.1, bf16[512,128]{1,0:T(8,128)(2,1)} %cent_ref.1, f32[1,128]{1,0:T(1,128)} %bitcast.5), custom_call_target="tpu_custom_call" | custom-call | tf_op jit(solution)/shard_map/pallas_call | solution.py:214
  3.9 11.8 %all-to-all-start = ((f32[16,4,128]{2,1,0:T(4,128)}), f32[16,4,128]{2,1,0:T(4,128)S(1)}, u32[]{:S(2)}, u32[]{:S(2)}) async-start(f32[16,4,128]{2,1,0:T(4,128)} %get-tuple-element.19), calls=%async_computation | async-start | bytes 65536 | tf_op jit(solution)/shard_map/all_to_all | solution.py:239
  15.8 0.0 copy-start
  15.8 1.0 copy-done
  16.8 0.0 copy-start.1
  16.8 0.9 copy-done.1
  17.7 0.0 copy-start.2
  17.7 0.7 copy-done.2
  18.4 0.0 copy-start.3
  18.4 0.7 copy-done.3
  19.0 0.8 shard_map.51
  19.9 3.0 %all-to-all-done.parts_ref = f32[16,4,128]{2,1,0:T(4,128)S(1)} async-done(((f32[16,4,128]{2,1,0:T(4,128)}), f32[16,4,128]{2,1,0:T(4,128)S(1)}, u32[]{:S(2)}, u32[]{:S(2)}) %all-to-all-start) | async-done | bytes 32800 | tf_op jit(solution)/shard_map/all_to_all | solution.py:239
  22.8 1.6 %shard_map.52 = (bf16[512,2048]{1,0:T(8,128)(2,1)S(1)}, f32[16,128]{1,0:T(8,128)S(1)}, f32[32,16,128]{2,1,0:T(8,128)S(1)}) custom-call(f32[16,4,128]{2,1,0:T(4,128)S(1)} %all-to-all-done.parts_ref, bf16[2048,128]{1,0:T(8,128)(2,1)S(1)} %get-tuple-element.21.tok_ref, bf16[512,128]{1,0:T(8,128)(2,1)S(1)} %get-tuple-element.22.half_ref, ...), custom_call_target="tpu_custom_call" | custom-call | tf_op jit(solution)/shard_map/pallas_call | solution.py:214
  24.5 19.2 %all_to_all.40.parts_ref = f32[32,16,128]{2,1,0:T(8,128)S(1)} all-to-all(f32[32,16,128]{2,1,0:T(8,128)S(1)} %get-tuple-element.25), channel_id=1, replica_groups=mesh['z'=8,'core'=2,'cent'=32] {'cent'}, dimensions={0} | all-to-all | bytes 524288 | tf_op jit(solution)/shard_map/all_to_all | solution.py:239
  43.6 0.7 shard_map.53
  44.3 14.4 %all_to_all.41.parts_ref = f32[16,4,128]{2,1,0:T(4,128)S(1)} all-to-all(f32[16,4,128]{2,1,0:T(4,128)S(1)} %get-tuple-element.28), channel_id=1, replica_groups=mesh['z'=8,'core'=2,'cent'=32] {'core','z'}, dimensions={0} | all-to-all | bytes 65536 | tf_op jit(solution)/shard_map/all_to_all | solution.py:239
  58.7 0.4 shard_map.54
  59.2 13.6 %all_to_all.42.parts_ref = f32[32,16,128]{2,1,0:T(8,128)S(1)} all-to-all(f32[32,16,128]{2,1,0:T(8,128)S(1)} %shard_map.54), channel_id=1, replica_groups=mesh['z'=8,'core'=2,'cent'=32] {'cent'}, dimensions={0} | all-to-all | bytes 524288 | tf_op jit(solution)/shard_map/all_to_all | solution.py:239
  72.8 0.7 shard_map.55
  73.5 13.1 %all_to_all.43.parts_ref = f32[16,4,128]{2,1,0:T(4,128)S(1)} all-to-all(f32[16,4,128]{2,1,0:T(4,128)S(1)} %shard_map.55), channel_id=1, replica_groups=mesh['z'=8,'core'=2,'cent'=32] {'core','z'}, dimensions={0} | all-to-all | bytes 65536 | tf_op jit(solution)/shard_map/all_to_all | solution.py:239
  86.6 0.4 shard_map.56
  87.0 13.6 %all_to_all.44.parts_ref = f32[32,16,128]{2,1,0:T(8,128)S(1)} all-to-all(f32[32,16,128]{2,1,0:T(8,128)S(1)} %get-tuple-element.30), channel_id=1, replica_groups=mesh['z'=8,'core'=2,'cent'=32] {'cent'}, dimensions={0} | all-to-all | bytes 524288 | tf_op jit(solution)/shard_map/all_to_all | solution.py:239
  100.7 0.9 shard_map.57
  101.5 16.9 %all_to_all.45.parts_ref = f32[16,40,128]{2,1,0:T(8,128)S(1)} all-to-all(f32[16,40,128]{2,1,0:T(8,128)S(1)} %shard_map.57), channel_id=1, replica_groups=mesh['z'=8,'core'=2,'cent'=32] {'core','z'}, dimensions={0} | all-to-all | bytes 655360 | tf_op jit(solution)/shard_map/all_to_all | solution.py:239
  118.4 0.1 shard_map.58
  118.5 12.1 %all_to_all.46 = f32[8,32,128]{2,1,0:T(8,128)S(1)} all-to-all(f32[8,32,128]{2,1,0:T(8,128)S(1)} %get-tuple-element.32), channel_id=1, replica_groups=mesh['z'=8,'core'=2,'cent'=32] {'z'}, dimensions={0} | all-to-all | bytes 262144 | tf_op jit(solution)/shard_map/all_to_all | solution.py:239
  130.6 3.9 %all-gather = f32[16,32,128]{2,1,0:T(8,128)S(1)} all-gather(f32[8,32,128]{2,1,0:T(8,128)S(1)} %all_to_all.46), channel_id=2, replica_groups=mesh['z'=8,'core'=2,'cent'=32] {'core'}, dimensions={0}, use_global_device_ids=true | all-gather | bytes 393216 | tf_op jit(solution)/shard_map/all_gather | solution.py:304
  134.5 0.7 shard_map.59
Async XLA Ops:
  3.9 18.9 %all-to-all-start = ((f32[16,4,128]{2,1,0:T(4,128)}), f32[16,4,128]{2,1,0:T(4,128)S(1)}, u32[]{:S(2)}, u32[]{:S(2)}) async-start(f32[16,4,128]{2,1,0:T(4,128)} %get-tuple-element.19), calls=%async_computation | async-start | bytes 65536 | tf_op jit(solution)/shard_map/all_to_all | solution.py:239
  15.8 1.0 copy-start
  16.8 0.9 copy-start.1
  17.7 0.7 copy-start.2
  18.4 0.7 copy-start.3

commit v8 on v7

--- a/solution.py
+++ b/solution.py
@@ -191,10 +191,10 @@
 
 
 def finish(cent_ref, mass_ref, cent_hbm, mass_hbm, sems):
-    cores = cent_ref.shape[0]
-    stores = [pltpu.make_async_copy(mass_ref, mass_hbm, sems.at[cores])]
-    for c in range(cores):
-        stores.append(pltpu.make_async_copy(cent_ref.at[c], cent_hbm.at[c], sems.at[c]))
+    stores = [
+        pltpu.make_async_copy(cent_ref, cent_hbm, sems.at[0]),
+        pltpu.make_async_copy(mass_ref, mass_hbm, sems.at[1]),
+    ]
     for store in stores:
         store.start()
     for store in stores:
@@ -225,8 +225,7 @@
 
 
 def shards(tokens, centroids, diagonal_factors):
-    chips, cores, cent = (lax.axis_size(axis) for axis in ("z", "core", "cent"))
-    dp = chips * cores
+    dp, cent = lax.axis_size(DP), lax.axis_size("cent")
     tok_local, dim = tokens.shape
     cent_local = centroids.shape[0]
     cent_count = cent_local * cent
@@ -297,17 +296,16 @@
     )
     copies, masses = run(
         functools.partial(divide, rows, ratio),
-        [((chips, rows, dim), F32), (by_cent, F32)],
+        [((dp, rows, dim), F32), (by_cent, F32)],
         over(DP, copies),
         scale,
     )
-    halves = lax.all_gather(over("z", copies), "core")
     new_centroids, masses = run(
         finish,
-        [((cores, chips, rows, dim), F32), (by_cent, F32)],
-        halves,
+        [((dp, rows, dim), F32), (by_cent, F32)],
+        over(DP, copies),
         masses,
-        scratch=[pltpu.SemaphoreType.DMA((cores + 1,))],
+        scratch=[pltpu.SemaphoreType.DMA((2,))],
         out_place=pltpu.HBM,
     )
     return (new_centroids.reshape(cent_local, dim), masses.reshape(cent_local))

time: 136 us -> 134 us (0.985)
  blocking collectives: 107 us -> 105 us
    all_gather x1 -> x0, blocking collectives: 3.89 us -> none  [shards(): halves = lax.all_gather(over('z', copies), 'core')]
    all_to_all x7, blocking collectives: 103 us -> 105 us  [over(): return lax.all_to_all(copies, axis, 0, 0)]
where the time goes in v8:
time: 134 us
  blocking collectives  105 us (78%)
  starting transfers between devices  11.8 us (9%)
  Pallas kernels  9.59 us (7%)
  local copies, waits for them, and re-layouts  3.27 us (2%)
  waiting for transfers between devices  2.96 us (2%)
    all_to_all x7, blocking collectives, over(): return lax.all_to_all(copies, axis, 0, 0)  105 us
    all_to_all x1, starting transfers between devices, over(): return lax.all_to_all(copies, axis, 0, 0)  11.8 us
    pallas_call x10, Pallas kernels, run(): pl.pallas_call(kernel, out_shape=[jax.ShapeDtypeStruct(shape, kind) for s...  9.59 us
    unnamed x8, local copies, waits for them, and re-layouts  3.27 us
    all_to_all x1, waiting for transfers between devices, over(): return lax.all_to_all(copies, axis, 0, 0)  2.96 us
  transfers between devices with their start and end apart: 1, of which 1 were waited for; matrix products, arithmetic and copies ran while one was open for 0% of the time, Pallas kernels for 1%

profile of v8, /device:TPU:1, one launch (start us, length us, event | category | flops | bytes accessed | tf_op | source)
XLA Modules:
  0.0 133.7 jit_solution(17145055028579680210)
XLA Ops:
  0.6 3.3 %shard_map.50 = (f32[16,4,128]{2,1,0:T(4,128)}, f32[8,128]{1,0:T(8,128)}) custom-call(bf16[2048,128]{1,0:T(8,128)(2,1)} %tok_ref.1, bf16[512,128]{1,0:T(8,128)(2,1)} %cent_ref.1, f32[1,128]{1,0:T(1,128)} %bitcast.3), custom_call_target="tpu_custom_call" | custom-call | tf_op jit(solution)/shard_map/pallas_call | solution.py:214
  3.9 11.8 %all-to-all-start = ((f32[16,4,128]{2,1,0:T(4,128)}), f32[16,4,128]{2,1,0:T(4,128)S(1)}, u32[]{:S(2)}, u32[]{:S(2)}) async-start(f32[16,4,128]{2,1,0:T(4,128)} %get-tuple-element.19), calls=%async_computation | async-start | bytes 65536 | tf_op jit(solution)/shard_map/all_to_all | solution.py:238
  15.8 0.0 copy-start
  15.8 1.0 copy-done
  16.8 0.0 copy-start.1
  16.8 0.9 copy-done.1
  17.7 0.0 copy-start.2
  17.7 0.7 copy-done.2
  18.4 0.0 copy-start.3
  18.4 0.7 copy-done.3
  19.0 0.8 shard_map.51
  19.9 3.0 %all-to-all-done.parts_ref = f32[16,4,128]{2,1,0:T(4,128)S(1)} async-done(((f32[16,4,128]{2,1,0:T(4,128)}), f32[16,4,128]{2,1,0:T(4,128)S(1)}, u32[]{:S(2)}, u32[]{:S(2)}) %all-to-all-start) | async-done | bytes 32800 | tf_op jit(solution)/shard_map/all_to_all | solution.py:238
  22.8 1.6 %shard_map.52 = (bf16[512,2048]{1,0:T(8,128)(2,1)S(1)}, f32[16,128]{1,0:T(8,128)S(1)}, f32[32,16,128]{2,1,0:T(8,128)S(1)}) custom-call(f32[16,4,128]{2,1,0:T(4,128)S(1)} %all-to-all-done.parts_ref, bf16[2048,128]{1,0:T(8,128)(2,1)S(1)} %get-tuple-element.21.tok_ref, bf16[512,128]{1,0:T(8,128)(2,1)S(1)} %get-tuple-element.22.half_ref, ...), custom_call_target="tpu_custom_call" | custom-call | tf_op jit(solution)/shard_map/pallas_call | solution.py:214
  24.5 19.2 %all_to_all.40.parts_ref = f32[32,16,128]{2,1,0:T(8,128)S(1)} all-to-all(f32[32,16,128]{2,1,0:T(8,128)S(1)} %get-tuple-element.25), channel_id=1, replica_groups=mesh['z'=8,'core'=2,'cent'=32] {'cent'}, dimensions={0} | all-to-all | bytes 524288 | tf_op jit(solution)/shard_map/all_to_all | solution.py:238
  43.6 0.7 shard_map.53
  44.3 14.4 %all_to_all.41.parts_ref = f32[16,4,128]{2,1,0:T(4,128)S(1)} all-to-all(f32[16,4,128]{2,1,0:T(4,128)S(1)} %get-tuple-element.28), channel_id=1, replica_groups=mesh['z'=8,'core'=2,'cent'=32] {'core','z'}, dimensions={0} | all-to-all | bytes 65536 | tf_op jit(solution)/shard_map/all_to_all | solution.py:238
  58.7 0.4 shard_map.54
  59.2 13.6 %all_to_all.42.parts_ref = f32[32,16,128]{2,1,0:T(8,128)S(1)} all-to-all(f32[32,16,128]{2,1,0:T(8,128)S(1)} %shard_map.54), channel_id=1, replica_groups=mesh['z'=8,'core'=2,'cent'=32] {'cent'}, dimensions={0} | all-to-all | bytes 524288 | tf_op jit(solution)/shard_map/all_to_all | solution.py:238
  72.8 0.7 shard_map.55
  73.5 13.1 %all_to_all.43.parts_ref = f32[16,4,128]{2,1,0:T(4,128)S(1)} all-to-all(f32[16,4,128]{2,1,0:T(4,128)S(1)} %shard_map.55), channel_id=1, replica_groups=mesh['z'=8,'core'=2,'cent'=32] {'core','z'}, dimensions={0} | all-to-all | bytes 65536 | tf_op jit(solution)/shard_map/all_to_all | solution.py:238
  86.6 0.4 shard_map.56
  87.0 13.6 %all_to_all.44.parts_ref = f32[32,16,128]{2,1,0:T(8,128)S(1)} all-to-all(f32[32,16,128]{2,1,0:T(8,128)S(1)} %get-tuple-element.30), channel_id=1, replica_groups=mesh['z'=8,'core'=2,'cent'=32] {'cent'}, dimensions={0} | all-to-all | bytes 524288 | tf_op jit(solution)/shard_map/all_to_all | solution.py:238
  100.7 0.9 shard_map.57
  101.5 16.9 %all_to_all.45.parts_ref = f32[16,40,128]{2,1,0:T(8,128)S(1)} all-to-all(f32[16,40,128]{2,1,0:T(8,128)S(1)} %shard_map.57), channel_id=1, replica_groups=mesh['z'=8,'core'=2,'cent'=32] {'core','z'}, dimensions={0} | all-to-all | bytes 655360 | tf_op jit(solution)/shard_map/all_to_all | solution.py:238
  118.4 0.1 shard_map.58
  118.5 14.5 %all_to_all.46.cent_ref = f32[16,32,128]{2,1,0:T(8,128)S(1)} all-to-all(f32[16,32,128]{2,1,0:T(8,128)S(1)} %get-tuple-element.32), channel_id=1, replica_groups=mesh['z'=8,'core'=2,'cent'=32] {'core','z'}, dimensions={0} | all-to-all | bytes 524288 | tf_op jit(solution)/shard_map/all_to_all | solution.py:238
  133.0 0.7 shard_map.59
Async XLA Ops:
  3.9 18.9 %all-to-all-start = ((f32[16,4,128]{2,1,0:T(4,128)}), f32[16,4,128]{2,1,0:T(4,128)S(1)}, u32[]{:S(2)}, u32[]{:S(2)}) async-start(f32[16,4,128]{2,1,0:T(4,128)} %get-tuple-element.19), calls=%async_computation | async-start | bytes 65536 | tf_op jit(solution)/shard_map/all_to_all | solution.py:238
  15.8 1.0 copy-start
  16.8 0.9 copy-start.1
  17.7 0.7 copy-start.2
  18.4 0.7 copy-start.3

commit v9 on v8

--- a/solution.py
+++ b/solution.py
@@ -11,6 +11,7 @@
 
 LANES = 128
 TILE = 256
+PART = 4
 DP = ("core", "z")
 F32 = jnp.float32
 BF16 = jnp.bfloat16
@@ -170,24 +171,30 @@
         share = (kept_ref[:, at].astype(F32) * pair_of_rows(weight, k)).astype(BF16)
         term = plain(share, jnp.concatenate([tok_ref[at, :], ones], axis=1))
         total = term if total is None else total + term
-    chunks = out_ref.shape[0]
-    out_ref[:, :rows, :] = total[:, :LANES].reshape(chunks, rows, LANES)
-    groups, per = total.shape[0] // LANES, LANES // rows
-    mass = [total[g * LANES : (g + 1) * LANES, LANES:].T[:1] for g in range(groups)]
-    for k in range(chunks):
-        own = jnp.broadcast_to(mass[k // per], (8, LANES))
-        if k % per:
-            own = pltpu.roll(own, LANES - (k % per) * rows, 1)
-        out_ref[k, rows:, :] = jnp.concatenate(mass + [own[: 8 - groups]], axis=0)
-
-
-def divide(rows, ratio, parts_ref, scale_ref, out_ref, mass_ref):
+    chunks, blocks = out_ref.shape[0], rows // PART
+    out_ref[:, :blocks] = total[:, :LANES].reshape(chunks, blocks, PART, LANES)
+    mass = [
+        total[g * LANES : (g + 1) * LANES, LANES:].T[:1] for g in range(total.shape[0] // LANES)
+    ]
+    mass = jnp.concatenate(mass, axis=0)
+    for g in range(mass.shape[0] // PART):
+        out_ref[:, blocks + g] = jnp.broadcast_to(
+            mass[None, g * PART : (g + 1) * PART], (chunks, PART, LANES)
+        )
+
+
+def divide(rows, ratio, parts_ref, scale_ref, out_ref, mass_ref, turned_ref):
     total = jnp.sum(parts_ref[...], axis=0)
-    groups = mass_ref.shape[0]
-    mass_ref[...] = total[rows : rows + groups] * scale_ref[...] / ratio
-    own = total[rows + groups : rows + groups + 1]
-    own = jnp.broadcast_to(own, (LANES, LANES)).T[:rows]
-    spread_out(out_ref, total[:rows] / own)
+    blocks = rows // PART
+    mass = total[blocks:].reshape(mass_ref.shape)
+    mass_ref[...] = mass * scale_ref[...] / ratio
+    me, per = lax.axis_index(DP), LANES // rows
+    group = jnp.broadcast_to(me // per, mass.shape)
+    row = lax.broadcasted_iota(jnp.int32, mass.shape, 0)
+    own = jnp.sum(jnp.where(row == group, mass, 0.0), axis=0, keepdims=True)
+    turned_ref[...] = jnp.broadcast_to(own, (LANES, LANES)).T
+    own = turned_ref[pl.ds(pl.multiple_of((me % per) * rows, rows), rows), :]
+    spread_out(out_ref, total[:blocks].reshape(rows, LANES) / own)
 
 
 def finish(cent_ref, mass_ref, cent_hbm, mass_hbm, sems):
@@ -285,7 +292,7 @@
     (copies,) = run(later_columns, [(to_dp, F32)], over("cent", copies), gain, kept)
     copies, scale = run(rows_of, rows_outs, over(DP, copies), gain, kept)
 
-    packed = (dp, rows + 8, LANES)
+    packed = (dp, rows // PART + by_cent[0] // PART, PART, LANES)
     (copies,) = run(
         functools.partial(numerators, rows),
         [(packed, F32)],
@@ -299,6 +306,7 @@
         [((dp, rows, dim), F32), (by_cent, F32)],
         over(DP, copies),
         scale,
+        scratch=[pltpu.VMEM((LANES, LANES), F32)],
     )
     new_centroids, masses = run(
         finish,

time: 134 us -> 134 us (level)
  no operation moved by 1% of the time
where the time goes in v9:
time: 134 us; the launch traced here: 133 us
  blocking collectives  105 us (78%)
  starting transfers between devices  11.8 us (9%)
  Pallas kernels  9.56 us (7%)
  local copies, waits for them, and re-layouts  3.27 us (2%)
  waiting for transfers between devices  2.96 us (2%)
    all_to_all x7, blocking collectives, over(): return lax.all_to_all(copies, axis, 0, 0)  105 us
    all_to_all x1, starting transfers between devices, over(): return lax.all_to_all(copies, axis, 0, 0)  11.8 us
    pallas_call x10, Pallas kernels, run(): pl.pallas_call(kernel, out_shape=[jax.ShapeDtypeStruct(shape, kind) for s...  9.56 us
    unnamed x8, local copies, waits for them, and re-layouts  3.27 us
    all_to_all x1, waiting for transfers between devices, over(): return lax.all_to_all(copies, axis, 0, 0)  2.96 us
  transfers between devices with their start and end apart: 1, of which 1 were waited for; matrix products, arithmetic and copies ran while one was open for 0% of the time, Pallas kernels for 1%

profile of v9, /device:TPU:1, one launch (start us, length us, event | category | flops | bytes accessed | tf_op | source)
XLA Modules:
  0.0 133.0 jit_solution(3684733468939641130)
XLA Ops:
  0.6 3.3 %shard_map.50 = (f32[16,4,128]{2,1,0:T(4,128)}, f32[8,128]{1,0:T(8,128)}) custom-call(bf16[2048,128]{1,0:T(8,128)(2,1)} %tok_ref.1, bf16[512,128]{1,0:T(8,128)(2,1)} %cent_ref.1, f32[1,128]{1,0:T(1,128)} %bitcast.3), custom_call_target="tpu_custom_call" | custom-call | tf_op jit(solution)/shard_map/pallas_call | solution.py:221
  3.9 11.8 %all-to-all-start = ((f32[16,4,128]{2,1,0:T(4,128)}), f32[16,4,128]{2,1,0:T(4,128)S(1)}, u32[]{:S(2)}, u32[]{:S(2)}) async-start(f32[16,4,128]{2,1,0:T(4,128)} %get-tuple-element.19), calls=%async_computation | async-start | bytes 65536 | tf_op jit(solution)/shard_map/all_to_all | solution.py:245
  15.8 0.0 copy-start
  15.8 1.0 copy-done
  16.8 0.0 copy-start.1
  16.8 0.9 copy-done.1
  17.7 0.0 copy-start.2
  17.7 0.7 copy-done.2
  18.4 0.0 copy-start.3
  18.4 0.7 copy-done.3
  19.0 0.8 shard_map.51
  19.9 3.0 %all-to-all-done.parts_ref = f32[16,4,128]{2,1,0:T(4,128)S(1)} async-done(((f32[16,4,128]{2,1,0:T(4,128)}), f32[16,4,128]{2,1,0:T(4,128)S(1)}, u32[]{:S(2)}, u32[]{:S(2)}) %all-to-all-start) | async-done | bytes 32800 | tf_op jit(solution)/shard_map/all_to_all | solution.py:245
  22.8 1.6 %shard_map.52 = (bf16[512,2048]{1,0:T(8,128)(2,1)S(1)}, f32[16,128]{1,0:T(8,128)S(1)}, f32[32,16,128]{2,1,0:T(8,128)S(1)}) custom-call(f32[16,4,128]{2,1,0:T(4,128)S(1)} %all-to-all-done.parts_ref, bf16[2048,128]{1,0:T(8,128)(2,1)S(1)} %get-tuple-element.21.tok_ref, bf16[512,128]{1,0:T(8,128)(2,1)S(1)} %get-tuple-element.22.half_ref, ...), custom_call_target="tpu_custom_call" | custom-call | tf_op jit(solution)/shard_map/pallas_call | solution.py:221
  24.5 19.2 %all_to_all.40.parts_ref = f32[32,16,128]{2,1,0:T(8,128)S(1)} all-to-all(f32[32,16,128]{2,1,0:T(8,128)S(1)} %get-tuple-element.25), channel_id=1, replica_groups=mesh['z'=8,'core'=2,'cent'=32] {'cent'}, dimensions={0} | all-to-all | bytes 524288 | tf_op jit(solution)/shard_map/all_to_all | solution.py:245
  43.6 0.7 shard_map.53
  44.3 14.4 %all_to_all.41.parts_ref = f32[16,4,128]{2,1,0:T(4,128)S(1)} all-to-all(f32[16,4,128]{2,1,0:T(4,128)S(1)} %get-tuple-element.28), channel_id=1, replica_groups=mesh['z'=8,'core'=2,'cent'=32] {'core','z'}, dimensions={0} | all-to-all | bytes 65536 | tf_op jit(solution)/shard_map/all_to_all | solution.py:245
  58.7 0.4 shard_map.54
  59.2 13.6 %all_to_all.42.parts_ref = f32[32,16,128]{2,1,0:T(8,128)S(1)} all-to-all(f32[32,16,128]{2,1,0:T(8,128)S(1)} %shard_map.54), channel_id=1, replica_groups=mesh['z'=8,'core'=2,'cent'=32] {'cent'}, dimensions={0} | all-to-all | bytes 524288 | tf_op jit(solution)/shard_map/all_to_all | solution.py:245
  72.8 0.7 shard_map.55
  73.5 13.1 %all_to_all.43.parts_ref = f32[16,4,128]{2,1,0:T(4,128)S(1)} all-to-all(f32[16,4,128]{2,1,0:T(4,128)S(1)} %shard_map.55), channel_id=1, replica_groups=mesh['z'=8,'core'=2,'cent'=32] {'core','z'}, dimensions={0} | all-to-all | bytes 65536 | tf_op jit(solution)/shard_map/all_to_all | solution.py:245
  86.6 0.4 shard_map.56
  87.0 13.6 %all_to_all.44.parts_ref = f32[32,16,128]{2,1,0:T(8,128)S(1)} all-to-all(f32[32,16,128]{2,1,0:T(8,128)S(1)} %get-tuple-element.30), channel_id=1, replica_groups=mesh['z'=8,'core'=2,'cent'=32] {'cent'}, dimensions={0} | all-to-all | bytes 524288 | tf_op jit(solution)/shard_map/all_to_all | solution.py:245
  100.7 0.8 shard_map.57
  101.4 16.1 %all_to_all.45.parts_ref = f32[16,9,4,128]{3,2,1,0:T(4,128)S(1)} all-to-all(f32[16,9,4,128]{3,2,1,0:T(4,128)S(1)} %shard_map.57), channel_id=1, replica_groups=mesh['z'=8,'core'=2,'cent'=32] {'core','z'}, dimensions={0} | all-to-all | bytes 589824 | tf_op jit(solution)/shard_map/all_to_all | solution.py:245
  117.6 0.2 shard_map.58
  117.7 14.5 %all_to_all.46.cent_ref = f32[16,32,128]{2,1,0:T(8,128)S(1)} all-to-all(f32[16,32,128]{2,1,0:T(8,128)S(1)} %get-tuple-element.32), channel_id=1, replica_groups=mesh['z'=8,'core'=2,'cent'=32] {'core','z'}, dimensions={0} | all-to-all | bytes 524288 | tf_op jit(solution)/shard_map/all_to_all | solution.py:245
  132.3 0.7 shard_map.59
Async XLA Ops:
  3.9 18.9 %all-to-all-start = ((f32[16,4,128]{2,1,0:T(4,128)}), f32[16,4,128]{2,1,0:T(4,128)S(1)}, u32[]{:S(2)}, u32[]{:S(2)}) async-start(f32[16,4,128]{2,1,0:T(4,128)} %get-tuple-element.19), calls=%async_computation | async-start | bytes 65536 | tf_op jit(solution)/shard_map/all_to_all | solution.py:245
  15.8 1.0 copy-start
  16.8 0.9 copy-start.1
  17.7 0.7 copy-start.2
  18.4 0.7 copy-start.3

commit v10 on v9

--- a/solution.py
+++ b/solution.py
@@ -12,6 +12,7 @@
 LANES = 128
 TILE = 256
 PART = 4
+STORES = 4
 DP = ("core", "z")
 F32 = jnp.float32
 BF16 = jnp.bfloat16
@@ -198,10 +199,11 @@
 
 
 def finish(cent_ref, mass_ref, cent_hbm, mass_hbm, sems):
-    stores = [
-        pltpu.make_async_copy(cent_ref, cent_hbm, sems.at[0]),
-        pltpu.make_async_copy(mass_ref, mass_hbm, sems.at[1]),
-    ]
+    stores = [pltpu.make_async_copy(mass_ref, mass_hbm, sems.at[STORES])]
+    share = cent_ref.shape[0] // STORES
+    for k in range(STORES):
+        at = pl.ds(k * share, share)
+        stores.append(pltpu.make_async_copy(cent_ref.at[at], cent_hbm.at[at], sems.at[k]))
     for store in stores:
         store.start()
     for store in stores:
@@ -313,7 +315,7 @@
         [((dp, rows, dim), F32), (by_cent, F32)],
         over(DP, copies),
         masses,
-        scratch=[pltpu.SemaphoreType.DMA((2,))],
+        scratch=[pltpu.SemaphoreType.DMA((STORES + 1,))],
         out_place=pltpu.HBM,
     )
     return (new_centroids.reshape(cent_local, dim), masses.reshape(cent_local))

time: 134 us -> 134 us (level)
  no operation moved by 1% of the time
where the time goes in v10:
time: 134 us; the launch traced here: 133 us
  blocking collectives  105 us (78%)
  starting transfers between devices  11.8 us (9%)
  Pallas kernels  9.58 us (7%)
  local copies, waits for them, and re-layouts  3.27 us (2%)
  waiting for transfers between devices  2.96 us (2%)
    all_to_all x7, blocking collectives, over(): return lax.all_to_all(copies, axis, 0, 0)  105 us
    all_to_all x1, starting transfers between devices, over(): return lax.all_to_all(copies, axis, 0, 0)  11.8 us
    pallas_call x10, Pallas kernels, run(): pl.pallas_call(kernel, out_shape=[jax.ShapeDtypeStruct(shape, kind) for s...  9.58 us
    unnamed x8, local copies, waits for them, and re-layouts  3.27 us
    all_to_all x1, waiting for transfers between devices, over(): return lax.all_to_all(copies, axis, 0, 0)  2.96 us
  transfers between devices with their start and end apart: 1, of which 1 were waited for; matrix products, arithmetic and copies ran while one was open for 0% of the time, Pallas kernels for 1%

profile of v10, /device:TPU:1, one launch (start us, length us, event | category | flops | bytes accessed | tf_op | source)
XLA Modules:
  0.0 133.0 jit_solution(13965960458414560328)
XLA Ops:
  0.6 3.3 %shard_map.50 = (f32[16,4,128]{2,1,0:T(4,128)}, f32[8,128]{1,0:T(8,128)}) custom-call(bf16[2048,128]{1,0:T(8,128)(2,1)} %tok_ref.1, bf16[512,128]{1,0:T(8,128)(2,1)} %cent_ref.1, f32[1,128]{1,0:T(1,128)} %bitcast.3), custom_call_target="tpu_custom_call" | custom-call | tf_op jit(solution)/shard_map/pallas_call | solution.py:223
  3.9 11.8 %all-to-all-start = ((f32[16,4,128]{2,1,0:T(4,128)}), f32[16,4,128]{2,1,0:T(4,128)S(1)}, u32[]{:S(2)}, u32[]{:S(2)}) async-start(f32[16,4,128]{2,1,0:T(4,128)} %get-tuple-element.19), calls=%async_computation | async-start | bytes 65536 | tf_op jit(solution)/shard_map/all_to_all | solution.py:247
  15.8 0.0 copy-start
  15.8 1.0 copy-done
  16.8 0.0 copy-start.1
  16.8 0.9 copy-done.1
  17.7 0.0 copy-start.2
  17.7 0.7 copy-done.2
  18.4 0.0 copy-start.3
  18.4 0.7 copy-done.3
  19.0 0.8 shard_map.51
  19.9 3.0 %all-to-all-done.parts_ref = f32[16,4,128]{2,1,0:T(4,128)S(1)} async-done(((f32[16,4,128]{2,1,0:T(4,128)}), f32[16,4,128]{2,1,0:T(4,128)S(1)}, u32[]{:S(2)}, u32[]{:S(2)}) %all-to-all-start) | async-done | bytes 32800 | tf_op jit(solution)/shard_map/all_to_all | solution.py:247
  22.8 1.6 %shard_map.52 = (bf16[512,2048]{1,0:T(8,128)(2,1)S(1)}, f32[16,128]{1,0:T(8,128)S(1)}, f32[32,16,128]{2,1,0:T(8,128)S(1)}) custom-call(f32[16,4,128]{2,1,0:T(4,128)S(1)} %all-to-all-done.parts_ref, bf16[2048,128]{1,0:T(8,128)(2,1)S(1)} %get-tuple-element.21.tok_ref, bf16[512,128]{1,0:T(8,128)(2,1)S(1)} %get-tuple-element.22.half_ref, ...), custom_call_target="tpu_custom_call" | custom-call | tf_op jit(solution)/shard_map/pallas_call | solution.py:223
  24.5 19.2 %all_to_all.40.parts_ref = f32[32,16,128]{2,1,0:T(8,128)S(1)} all-to-all(f32[32,16,128]{2,1,0:T(8,128)S(1)} %get-tuple-element.25), channel_id=1, replica_groups=mesh['z'=8,'core'=2,'cent'=32] {'cent'}, dimensions={0} | all-to-all | bytes 524288 | tf_op jit(solution)/shard_map/all_to_all | solution.py:247
  43.6 0.7 shard_map.53
  44.3 14.4 %all_to_all.41.parts_ref = f32[16,4,128]{2,1,0:T(4,128)S(1)} all-to-all(f32[16,4,128]{2,1,0:T(4,128)S(1)} %get-tuple-element.28), channel_id=1, replica_groups=mesh['z'=8,'core'=2,'cent'=32] {'core','z'}, dimensions={0} | all-to-all | bytes 65536 | tf_op jit(solution)/shard_map/all_to_all | solution.py:247
  58.7 0.4 shard_map.54
  59.2 13.6 %all_to_all.42.parts_ref = f32[32,16,128]{2,1,0:T(8,128)S(1)} all-to-all(f32[32,16,128]{2,1,0:T(8,128)S(1)} %shard_map.54), channel_id=1, replica_groups=mesh['z'=8,'core'=2,'cent'=32] {'cent'}, dimensions={0} | all-to-all | bytes 524288 | tf_op jit(solution)/shard_map/all_to_all | solution.py:247
  72.8 0.7 shard_map.55
  73.5 13.1 %all_to_all.43.parts_ref = f32[16,4,128]{2,1,0:T(4,128)S(1)} all-to-all(f32[16,4,128]{2,1,0:T(4,128)S(1)} %shard_map.55), channel_id=1, replica_groups=mesh['z'=8,'core'=2,'cent'=32] {'core','z'}, dimensions={0} | all-to-all | bytes 65536 | tf_op jit(solution)/shard_map/all_to_all | solution.py:247
  86.6 0.4 shard_map.56
  87.0 13.6 %all_to_all.44.parts_ref = f32[32,16,128]{2,1,0:T(8,128)S(1)} all-to-all(f32[32,16,128]{2,1,0:T(8,128)S(1)} %get-tuple-element.30), channel_id=1, replica_groups=mesh['z'=8,'core'=2,'cent'=32] {'cent'}, dimensions={0} | all-to-all | bytes 524288 | tf_op jit(solution)/shard_map/all_to_all | solution.py:247
  100.7 0.8 shard_map.57
  101.4 16.1 %all_to_all.45.parts_ref = f32[16,9,4,128]{3,2,1,0:T(4,128)S(1)} all-to-all(f32[16,9,4,128]{3,2,1,0:T(4,128)S(1)} %shard_map.57), channel_id=1, replica_groups=mesh['z'=8,'core'=2,'cent'=32] {'core','z'}, dimensions={0} | all-to-all | bytes 589824 | tf_op jit(solution)/shard_map/all_to_all | solution.py:247
  117.6 0.2 shard_map.58
  117.7 14.5 %all_to_all.46.cent_ref = f32[16,32,128]{2,1,0:T(8,128)S(1)} all-to-all(f32[16,32,128]{2,1,0:T(8,128)S(1)} %get-tuple-element.32), channel_id=1, replica_groups=mesh['z'=8,'core'=2,'cent'=32] {'core','z'}, dimensions={0} | all-to-all | bytes 524288 | tf_op jit(solution)/shard_map/all_to_all | solution.py:247
  132.3 0.7 shard_map.59
Async XLA Ops:
  3.9 18.9 %all-to-all-start = ((f32[16,4,128]{2,1,0:T(4,128)}), f32[16,4,128]{2,1,0:T(4,128)S(1)}, u32[]{:S(2)}, u32[]{:S(2)}) async-start(f32[16,4,128]{2,1,0:T(4,128)} %get-tuple-element.19), calls=%async_computation | async-start | bytes 65536 | tf_op jit(solution)/shard_map/all_to_all | solution.py:247
  15.8 1.0 copy-start
  16.8 0.9 copy-start.1
  17.7 0.7 copy-start.2
  18.4 0.7 copy-start.3

commit v11 on v9

--- a/solution.py
+++ b/solution.py
@@ -194,7 +194,7 @@
     own = jnp.sum(jnp.where(row == group, mass, 0.0), axis=0, keepdims=True)
     turned_ref[...] = jnp.broadcast_to(own, (LANES, LANES)).T
     own = turned_ref[pl.ds(pl.multiple_of((me % per) * rows, rows), rows), :]
-    spread_out(out_ref, total[:blocks].reshape(rows, LANES) / own)
+    spread_out(out_ref, (total[:blocks].reshape(rows, LANES) / own).reshape(blocks, PART, LANES))
 
 
 def finish(cent_ref, mass_ref, cent_hbm, mass_hbm, sems):
@@ -303,14 +303,14 @@
     )
     copies, masses = run(
         functools.partial(divide, rows, ratio),
-        [((dp, rows, dim), F32), (by_cent, F32)],
+        [((dp, rows // PART, PART, dim), F32), (by_cent, F32)],
         over(DP, copies),
         scale,
         scratch=[pltpu.VMEM((LANES, LANES), F32)],
     )
     new_centroids, masses = run(
         finish,
-        [((dp, rows, dim), F32), (by_cent, F32)],
+        [((dp, rows // PART, PART, dim), F32), (by_cent, F32)],
         over(DP, copies),
         masses,
         scratch=[pltpu.SemaphoreType.DMA((2,))],

time: 134 us -> 134 us (level)
  no operation moved by 1% of the time
where the time goes in v11:
time: 134 us; the launch traced here: 133 us
  blocking collectives  105 us (78%)
  starting transfers between devices  11.8 us (9%)
  Pallas kernels  9.58 us (7%)
  local copies, waits for them, and re-layouts  3.27 us (2%)
  waiting for transfers between devices  2.96 us (2%)
    all_to_all x7, blocking collectives, over(): return lax.all_to_all(copies, axis, 0, 0)  105 us
    all_to_all x1, starting transfers between devices, over(): return lax.all_to_all(copies, axis, 0, 0)  11.8 us
    pallas_call x10, Pallas kernels, run(): pl.pallas_call(kernel, out_shape=[jax.ShapeDtypeStruct(shape, kind) for s...  9.58 us
    unnamed x8, local copies, waits for them, and re-layouts  3.27 us
    all_to_all x1, waiting for transfers between devices, over(): return lax.all_to_all(copies, axis, 0, 0)  2.96 us
  transfers between devices with their start and end apart: 1, of which 1 were waited for; matrix products, arithmetic and copies ran while one was open for 0% of the time, Pallas kernels for 1%

profile of v11, /device:TPU:1, one launch (start us, length us, event | category | flops | bytes accessed | tf_op | source)
XLA Modules:
  0.0 133.0 jit_solution(2066285290407292545)
XLA Ops:
  0.6 3.3 %shard_map.50 = (f32[16,4,128]{2,1,0:T(4,128)}, f32[8,128]{1,0:T(8,128)}) custom-call(bf16[2048,128]{1,0:T(8,128)(2,1)} %tok_ref.1, bf16[512,128]{1,0:T(8,128)(2,1)} %cent_ref.1, f32[1,128]{1,0:T(1,128)} %bitcast.3), custom_call_target="tpu_custom_call" | custom-call | tf_op jit(solution)/shard_map/pallas_call | solution.py:221
  3.9 11.8 %all-to-all-start = ((f32[16,4,128]{2,1,0:T(4,128)}), f32[16,4,128]{2,1,0:T(4,128)S(1)}, u32[]{:S(2)}, u32[]{:S(2)}) async-start(f32[16,4,128]{2,1,0:T(4,128)} %get-tuple-element.19), calls=%async_computation | async-start | bytes 65536 | tf_op jit(solution)/shard_map/all_to_all | solution.py:245
  15.8 0.0 copy-start
  15.8 1.0 copy-done
  16.8 0.0 copy-start.1
  16.8 0.9 copy-done.1
  17.7 0.0 copy-start.2
  17.7 0.7 copy-done.2
  18.4 0.0 copy-start.3
  18.4 0.7 copy-done.3
  19.0 0.8 shard_map.51
  19.9 3.0 %all-to-all-done.parts_ref = f32[16,4,128]{2,1,0:T(4,128)S(1)} async-done(((f32[16,4,128]{2,1,0:T(4,128)}), f32[16,4,128]{2,1,0:T(4,128)S(1)}, u32[]{:S(2)}, u32[]{:S(2)}) %all-to-all-start) | async-done | bytes 32800 | tf_op jit(solution)/shard_map/all_to_all | solution.py:245
  22.8 1.6 %shard_map.52 = (bf16[512,2048]{1,0:T(8,128)(2,1)S(1)}, f32[16,128]{1,0:T(8,128)S(1)}, f32[32,16,128]{2,1,0:T(8,128)S(1)}) custom-call(f32[16,4,128]{2,1,0:T(4,128)S(1)} %all-to-all-done.parts_ref, bf16[2048,128]{1,0:T(8,128)(2,1)S(1)} %get-tuple-element.21.tok_ref, bf16[512,128]{1,0:T(8,128)(2,1)S(1)} %get-tuple-element.22.half_ref, ...), custom_call_target="tpu_custom_call" | custom-call | tf_op jit(solution)/shard_map/pallas_call | solution.py:221
  24.5 19.2 %all_to_all.40.parts_ref = f32[32,16,128]{2,1,0:T(8,128)S(1)} all-to-all(f32[32,16,128]{2,1,0:T(8,128)S(1)} %get-tuple-element.25), channel_id=1, replica_groups=mesh['z'=8,'core'=2,'cent'=32] {'cent'}, dimensions={0} | all-to-all | bytes 524288 | tf_op jit(solution)/shard_map/all_to_all | solution.py:245
  43.6 0.7 shard_map.53
  44.3 14.4 %all_to_all.41.parts_ref = f32[16,4,128]{2,1,0:T(4,128)S(1)} all-to-all(f32[16,4,128]{2,1,0:T(4,128)S(1)} %get-tuple-element.28), channel_id=1, replica_groups=mesh['z'=8,'core'=2,'cent'=32] {'core','z'}, dimensions={0} | all-to-all | bytes 65536 | tf_op jit(solution)/shard_map/all_to_all | solution.py:245
  58.7 0.4 shard_map.54
  59.2 13.6 %all_to_all.42.parts_ref = f32[32,16,128]{2,1,0:T(8,128)S(1)} all-to-all(f32[32,16,128]{2,1,0:T(8,128)S(1)} %shard_map.54), channel_id=1, replica_groups=mesh['z'=8,'core'=2,'cent'=32] {'cent'}, dimensions={0} | all-to-all | bytes 524288 | tf_op jit(solution)/shard_map/all_to_all | solution.py:245
  72.8 0.7 shard_map.55
  73.5 13.1 %all_to_all.43.parts_ref = f32[16,4,128]{2,1,0:T(4,128)S(1)} all-to-all(f32[16,4,128]{2,1,0:T(4,128)S(1)} %shard_map.55), channel_id=1, replica_groups=mesh['z'=8,'core'=2,'cent'=32] {'core','z'}, dimensions={0} | all-to-all | bytes 65536 | tf_op jit(solution)/shard_map/all_to_all | solution.py:245
  86.6 0.4 shard_map.56
  87.0 13.6 %all_to_all.44.parts_ref = f32[32,16,128]{2,1,0:T(8,128)S(1)} all-to-all(f32[32,16,128]{2,1,0:T(8,128)S(1)} %get-tuple-element.30), channel_id=1, replica_groups=mesh['z'=8,'core'=2,'cent'=32] {'cent'}, dimensions={0} | all-to-all | bytes 524288 | tf_op jit(solution)/shard_map/all_to_all | solution.py:245
  100.7 0.8 shard_map.57
  101.4 16.1 %all_to_all.45.parts_ref = f32[16,9,4,128]{3,2,1,0:T(4,128)S(1)} all-to-all(f32[16,9,4,128]{3,2,1,0:T(4,128)S(1)} %shard_map.57), channel_id=1, replica_groups=mesh['z'=8,'core'=2,'cent'=32] {'core','z'}, dimensions={0} | all-to-all | bytes 589824 | tf_op jit(solution)/shard_map/all_to_all | solution.py:245
  117.6 0.2 shard_map.58
  117.8 14.5 %all_to_all.46.cent_ref = f32[16,8,4,128]{3,2,1,0:T(4,128)S(1)} all-to-all(f32[16,8,4,128]{3,2,1,0:T(4,128)S(1)} %get-tuple-element.32), channel_id=1, replica_groups=mesh['z'=8,'core'=2,'cent'=32] {'core','z'}, dimensions={0} | all-to-all | bytes 524288 | tf_op jit(solution)/shard_map/all_to_all | solution.py:245
  132.3 0.7 shard_map.59
Async XLA Ops:
  3.9 18.9 %all-to-all-start = ((f32[16,4,128]{2,1,0:T(4,128)}), f32[16,4,128]{2,1,0:T(4,128)S(1)}, u32[]{:S(2)}, u32[]{:S(2)}) async-start(f32[16,4,128]{2,1,0:T(4,128)} %get-tuple-element.19), calls=%async_computation | async-start | bytes 65536 | tf_op jit(solution)/shard_map/all_to_all | solution.py:245
  15.8 1.0 copy-start
  16.8 0.9 copy-start.1
  17.7 0.7 copy-start.2
  18.4 0.7 copy-start.3

commit v12 on v9

--- a/solution.py
+++ b/solution.py
@@ -13,6 +13,7 @@
 TILE = 256
 PART = 4
 DP = ("core", "z")
+CENT = ("y", "x")
 F32 = jnp.float32
 BF16 = jnp.bfloat16
 
@@ -232,7 +233,7 @@
 
 
 def shards(tokens, centroids, diagonal_factors):
-    dp, cent = lax.axis_size(DP), lax.axis_size("cent")
+    dp, cent = lax.axis_size(DP), lax.axis_size(CENT)
     tok_local, dim = tokens.shape
     cent_local = centroids.shape[0]
     cent_count = cent_local * cent
@@ -282,21 +283,21 @@
     copies, gain = run(
         second_columns,
         [(to_dp, F32), (by_tok, F32)],
-        over("cent", copies),
+        over(CENT, copies),
         top,
         kept,
     )
     rows_of = functools.partial(later_rows, ratio)
     rows_outs = [(to_cent, F32), (by_cent, F32)]
     (copies,) = run(rows_of, rows_outs[:1], over(DP, copies), gain, kept)
-    (copies,) = run(later_columns, [(to_dp, F32)], over("cent", copies), gain, kept)
+    (copies,) = run(later_columns, [(to_dp, F32)], over(CENT, copies), gain, kept)
     copies, scale = run(rows_of, rows_outs, over(DP, copies), gain, kept)
 
     packed = (dp, rows // PART + by_cent[0] // PART, PART, LANES)
     (copies,) = run(
         functools.partial(numerators, rows),
         [(packed, F32)],
-        over("cent", copies),
+        over(CENT, copies),
         gain,
         kept,
         near,
@@ -321,11 +322,11 @@
 
 def solution(mesh):
     dp, cent = mesh.devices.shape
-    split = Mesh(mesh.devices.reshape(dp // 2, 2, cent), ("z", "core", "cent"))
+    split = Mesh(mesh.devices.reshape(dp // 2, 2, 4, cent // 4), ("z", "core", "x", "y"))
     return jax.shard_map(
         shards,
         mesh=split,
-        in_specs=(P(("z", "core"), None), P("cent", None), P()),
-        out_specs=(P("cent", None), P("cent")),
+        in_specs=(P(("z", "core"), None), P(("x", "y"), None), P()),
+        out_specs=(P(("x", "y"), None), P(("x", "y"))),
         check_vma=False,
     )

time: 134 us -> 134 us (level)
  no operation moved by 1% of the time
where the time goes in v12:
time: 134 us; the launch traced here: 133 us
  blocking collectives  105 us (78%)
  starting transfers between devices  11.8 us (9%)
  Pallas kernels  9.56 us (7%)
  local copies, waits for them, and re-layouts  3.27 us (2%)
  waiting for transfers between devices  2.96 us (2%)
    all_to_all x7, blocking collectives, over(): return lax.all_to_all(copies, axis, 0, 0)  105 us
    all_to_all x1, starting transfers between devices, over(): return lax.all_to_all(copies, axis, 0, 0)  11.8 us
    pallas_call x10, Pallas kernels, run(): pl.pallas_call(kernel, out_shape=[jax.ShapeDtypeStruct(shape, kind) for s...  9.56 us
    unnamed x8, local copies, waits for them, and re-layouts  3.27 us
    all_to_all x1, waiting for transfers between devices, over(): return lax.all_to_all(copies, axis, 0, 0)  2.96 us
  transfers between devices with their start and end apart: 1, of which 1 were waited for; matrix products, arithmetic and copies ran while one was open for 0% of the time, Pallas kernels for 1%

profile of v12, /device:TPU:1, one launch (start us, length us, event | category | flops | bytes accessed | tf_op | source)
XLA Modules:
  0.0 133.1 jit_solution(11544351492060740817)
XLA Ops:
  0.6 3.3 %shard_map.50 = (f32[16,4,128]{2,1,0:T(4,128)}, f32[8,128]{1,0:T(8,128)}) custom-call(bf16[2048,128]{1,0:T(8,128)(2,1)} %tok_ref.1, bf16[512,128]{1,0:T(8,128)(2,1)} %cent_ref.1, f32[1,128]{1,0:T(1,128)} %bitcast.3), custom_call_target="tpu_custom_call" | custom-call | tf_op jit(solution)/shard_map/pallas_call | solution.py:222
  3.9 11.8 %all-to-all-start = ((f32[16,4,128]{2,1,0:T(4,128)}), f32[16,4,128]{2,1,0:T(4,128)S(1)}, u32[]{:S(2)}, u32[]{:S(2)}) async-start(f32[16,4,128]{2,1,0:T(4,128)} %get-tuple-element.19), calls=%async_computation | async-start | bytes 65536 | tf_op jit(solution)/shard_map/all_to_all | solution.py:246
  15.8 0.0 copy-start
  15.8 1.0 copy-done
  16.8 0.0 copy-start.1
  16.8 0.9 copy-done.1
  17.7 0.0 copy-start.2
  17.7 0.7 copy-done.2
  18.4 0.0 copy-start.3
  18.4 0.7 copy-done.3
  19.0 0.8 shard_map.51
  19.9 3.0 %all-to-all-done.parts_ref = f32[16,4,128]{2,1,0:T(4,128)S(1)} async-done(((f32[16,4,128]{2,1,0:T(4,128)}), f32[16,4,128]{2,1,0:T(4,128)S(1)}, u32[]{:S(2)}, u32[]{:S(2)}) %all-to-all-start) | async-done | bytes 32800 | tf_op jit(solution)/shard_map/all_to_all | solution.py:246
  22.8 1.6 %shard_map.52 = (bf16[512,2048]{1,0:T(8,128)(2,1)S(1)}, f32[16,128]{1,0:T(8,128)S(1)}, f32[32,16,128]{2,1,0:T(8,128)S(1)}) custom-call(f32[16,4,128]{2,1,0:T(4,128)S(1)} %all-to-all-done.parts_ref, bf16[2048,128]{1,0:T(8,128)(2,1)S(1)} %get-tuple-element.21.tok_ref, bf16[512,128]{1,0:T(8,128)(2,1)S(1)} %get-tuple-element.22.half_ref, ...), custom_call_target="tpu_custom_call" | custom-call | tf_op jit(solution)/shard_map/pallas_call | solution.py:222
  24.5 20.7 %all_to_all.40.parts_ref = f32[32,16,128]{2,1,0:T(8,128)S(1)} all-to-all(f32[32,16,128]{2,1,0:T(8,128)S(1)} %get-tuple-element.25), channel_id=1, replica_groups=mesh['z'=8,'core'=2,'x'=4,'y'=8] {'y','x'}, dimensions={0} | all-to-all | bytes 524288 | tf_op jit(solution)/shard_map/all_to_all | solution.py:246
  45.2 0.7 shard_map.53
  45.9 13.4 %all_to_all.41.parts_ref = f32[16,4,128]{2,1,0:T(4,128)S(1)} all-to-all(f32[16,4,128]{2,1,0:T(4,128)S(1)} %get-tuple-element.28), channel_id=1, replica_groups=mesh['z'=8,'core'=2,'x'=4,'y'=8] {'core','z'}, dimensions={0} | all-to-all | bytes 65536 | tf_op jit(solution)/shard_map/all_to_all | solution.py:246
  59.3 0.4 shard_map.54
  59.7 14.6 %all_to_all.42.parts_ref = f32[32,16,128]{2,1,0:T(8,128)S(1)} all-to-all(f32[32,16,128]{2,1,0:T(8,128)S(1)} %shard_map.54), channel_id=1, replica_groups=mesh['z'=8,'core'=2,'x'=4,'y'=8] {'y','x'}, dimensions={0} | all-to-all | bytes 524288 | tf_op jit(solution)/shard_map/all_to_all | solution.py:246
  74.3 0.7 shard_map.55
  75.0 11.8 %all_to_all.43.parts_ref = f32[16,4,128]{2,1,0:T(4,128)S(1)} all-to-all(f32[16,4,128]{2,1,0:T(4,128)S(1)} %shard_map.55), channel_id=1, replica_groups=mesh['z'=8,'core'=2,'x'=4,'y'=8] {'core','z'}, dimensions={0} | all-to-all | bytes 65536 | tf_op jit(solution)/shard_map/all_to_all | solution.py:246
  86.8 0.4 shard_map.56
  87.2 14.9 %all_to_all.44.parts_ref = f32[32,16,128]{2,1,0:T(8,128)S(1)} all-to-all(f32[32,16,128]{2,1,0:T(8,128)S(1)} %get-tuple-element.30), channel_id=1, replica_groups=mesh['z'=8,'core'=2,'x'=4,'y'=8] {'y','x'}, dimensions={0} | all-to-all | bytes 524288 | tf_op jit(solution)/shard_map/all_to_all | solution.py:246
  102.1 0.8 shard_map.57
  102.9 14.8 %all_to_all.45.parts_ref = f32[16,9,4,128]{3,2,1,0:T(4,128)S(1)} all-to-all(f32[16,9,4,128]{3,2,1,0:T(4,128)S(1)} %shard_map.57), channel_id=1, replica_groups=mesh['z'=8,'core'=2,'x'=4,'y'=8] {'core','z'}, dimensions={0} | all-to-all | bytes 589824 | tf_op jit(solution)/shard_map/all_to_all | solution.py:246
  117.7 0.2 shard_map.58
  117.9 14.5 %all_to_all.46.cent_ref = f32[16,32,128]{2,1,0:T(8,128)S(1)} all-to-all(f32[16,32,128]{2,1,0:T(8,128)S(1)} %get-tuple-element.32), channel_id=1, replica_groups=mesh['z'=8,'core'=2,'x'=4,'y'=8] {'core','z'}, dimensions={0} | all-to-all | bytes 524288 | tf_op jit(solution)/shard_map/all_to_all | solution.py:246
  132.4 0.7 shard_map.59
Async XLA Ops:
  3.9 18.9 %all-to-all-start = ((f32[16,4,128]{2,1,0:T(4,128)}), f32[16,4,128]{2,1,0:T(4,128)S(1)}, u32[]{:S(2)}, u32[]{:S(2)}) async-start(f32[16,4,128]{2,1,0:T(4,128)} %get-tuple-element.19), calls=%async_computation | async-start | bytes 65536 | tf_op jit(solution)/shard_map/all_to_all | solution.py:246
  15.8 1.0 copy-start
  16.8 0.9 copy-start.1
  17.7 0.7 copy-start.2
  18.4 0.7 copy-start.3
